TPU v7x, 32 devices: a whole 2x2x4 slice. The times are simulated.
32 devices in a mesh: dp: 8 (over z, x), tensor: 4 (over y, core).
Axes of the slice: x: 2, y: 2, z: 4, core: 2. Of those that a mesh axis runs over, the one named last changes fastest.
Arguments:
- inputs: bfloat16 [8, 3, 512, 1024], P('dp', None, 'tensor'), may hold values from -6 to 6
- lengths: int32 [8, 3], P('dp'), may hold values from 128 to 512, as said below
- cotangent: bfloat16 [8, 3, 512, 1024], P('dp', None, 'tensor'), may hold values from -6 to 6
- w_qkv: bfloat16 [1024, 3, 1024], P(None, None, 'tensor'), may hold values from -0.1875 to 0.1875
- b_query: bfloat16 [1024], P('tensor'), may hold values from -3 to 3
- b_value: bfloat16 [1024], P('tensor'), may hold values from -3 to 3
- w_out: bfloat16 [1024, 1024], P('tensor'), may hold values from -0.75 to 0.75
- b_out: bfloat16 [1024], replicated, may hold values from -3 to 3
- ln1_gain: bfloat16 [1024], replicated, may hold values from 0.5 to 1.5
- ln1_bias: bfloat16 [1024], replicated, may hold values from -3 to 3
- w_up: bfloat16 [1024, 4096], P(None, 'tensor'), may hold values from -0.1875 to 0.1875
- b_up: bfloat16 [4096], P('tensor'), may hold values from -3 to 3
- w_down: bfloat16 [4096, 1024], P('tensor'), may hold values from -0.09375 to 0.09375
- b_down: bfloat16 [1024], replicated, may hold values from -3 to 3
- ln2_gain: bfloat16 [1024], replicated, may hold values from 0.5 to 1.5
- ln2_bias: bfloat16 [1024], replicated, may hold values from -3 to 3
Outputs:
- output: bfloat16 [8, 3, 512, 1024], P('dp', None, 'tensor')
- grad_inputs: bfloat16 [8, 3, 512, 1024], P('dp', None, 'tensor')
- grad_qkv: float32 [1024, 3, 1024], P(None, None, 'tensor')
- grad_query_bias: float32 [1024], P('tensor')
- grad_value_bias: float32 [1024], P('tensor')
- grad_out: float32 [1024, 1024], P('tensor')
- grad_out_bias: float32 [1024], replicated
- grad_ln1_gain: float32 [1024], replicated
- grad_ln1_bias: float32 [1024], replicated
- grad_up: float32 [1024, 4096], P(None, 'tensor')
- grad_up_bias: float32 [4096], P('tensor')
- grad_down: float32 [4096, 1024], P('tensor')
- grad_down_bias: float32 [1024], replicated
- grad_ln2_gain: float32 [1024], replicated
- grad_ln2_bias: float32 [1024], replicated
Inputs may be any that keep to these rules, and one draw needn't show every extreme that they name: Each row of lengths has one entry equal to 512; a sequence fills the first lengths entries of its 512 slots, the rest is padding.
All inputs are finite; a program needn't handle non-finite values.
Results may differ from a plain program's by a relative error of at most 0.018.
Values may be sent and summed in bfloat16 or wider, within the bound.
A program may use at most 128 MiB of HBM per device.

v0:
```python
import jax
import jax.numpy as jnp
from jax import lax
from jax.sharding import PartitionSpec as P

HD = 64


EPSILON = 1e-05


def layer_norm(values, norm_gain, norm_shift):
    row_mean = jnp.mean(values, axis=-1, keepdims=True)
    centred = values - row_mean
    spread = jnp.mean(centred * centred, axis=-1, keepdims=True)
    return centred * lax.rsqrt(spread + EPSILON) * norm_gain + norm_shift


def exact_gelu(values):
    return jax.nn.gelu(values, approximate=False)


def attention_forward(queries, keys_low, values_low, key_mask):
    length_all = queries.shape[0]
    head_width = queries.shape[1]
    head_count = head_width // HD
    block_rows = min(512, length_all)
    blocks = length_all // block_rows
    score_scale = HD ** (-0.5)
    query_blocks = queries.reshape(blocks, block_rows, head_count, HD)
    key_heads = keys_low.reshape(length_all, head_count, HD)
    value_heads = values_low.reshape(length_all, head_count, HD)

    def one_block(query_block):
        scores = (
            jnp.einsum("qhd,khd->hqk", query_block, key_heads, preferred_element_type=jnp.float32)
            * score_scale
        )
        scores = jnp.where(key_mask[None, None, :], scores, -1e30)
        row_max = jnp.max(scores, axis=-1, keepdims=True)
        raw_weights = jnp.exp(scores - row_max)
        totals = jnp.sum(raw_weights, axis=-1, keepdims=True)
        probabilities = raw_weights / totals
        context = jnp.einsum(
            "hqk,khd->qhd",
            probabilities.astype(jnp.bfloat16),
            value_heads,
            preferred_element_type=jnp.float32,
        )
        return (context.astype(jnp.bfloat16), row_max[..., 0] + jnp.log(totals[..., 0]))

    context, log_totals = lax.map(one_block, query_blocks)
    return (context.reshape(length_all, head_width), log_totals)


def attention_backward(queries, keys_low, values_low, grad_context, key_mask, log_totals):
    length_all = queries.shape[0]
    head_width = queries.shape[1]
    head_count = head_width // HD
    block_rows = min(512, length_all)
    blocks = length_all // block_rows
    score_scale = HD ** (-0.5)
    query_blocks = queries.reshape(blocks, block_rows, head_count, HD)
    grad_blocks = grad_context.reshape(blocks, block_rows, head_count, HD)
    key_heads = keys_low.reshape(length_all, head_count, HD)
    value_heads = values_low.reshape(length_all, head_count, HD)

    def one_block(carried, block_item):
        grad_keys, grad_values = carried
        query_block, grad_block, log_block = block_item
        scores = (
            jnp.einsum("qhd,khd->hqk", query_block, key_heads, preferred_element_type=jnp.float32)
            * score_scale
        )
        scores = jnp.where(key_mask[None, None, :], scores, -1e30)
        probabilities = jnp.exp(scores - log_block[..., None])
        grad_values = grad_values + jnp.einsum(
            "hqk,qhd->khd",
            probabilities.astype(jnp.bfloat16),
            grad_block,
            preferred_element_type=jnp.float32,
        )
        grad_probs = jnp.einsum(
            "qhd,khd->hqk", grad_block, value_heads, preferred_element_type=jnp.float32
        )
        grad_scores = probabilities * (
            grad_probs - jnp.sum(probabilities * grad_probs, axis=-1, keepdims=True)
        )
        low_scores = grad_scores.astype(jnp.bfloat16)
        grad_query = (
            jnp.einsum("hqk,khd->qhd", low_scores, key_heads, preferred_element_type=jnp.float32)
            * score_scale
        )
        grad_keys = (
            grad_keys
            + jnp.einsum(
                "hqk,qhd->khd", low_scores, query_block, preferred_element_type=jnp.float32
            )
            * score_scale
        )
        return ((grad_keys, grad_values), grad_query)

    empty_keys = jnp.zeros((length_all, head_count, HD), jnp.float32)
    (grad_keys, grad_values), grad_queries = lax.scan(
        one_block, (empty_keys, empty_keys), (query_blocks, grad_blocks, log_totals)
    )
    return (
        grad_queries.reshape(length_all, head_width),
        grad_keys.reshape(length_all, head_width),
        grad_values.reshape(length_all, head_width),
    )


def per_device(
    inputs,
    lengths,
    cotangent,
    w_qkv,
    b_query,
    b_value,
    w_out,
    b_out,
    ln1_gain,
    ln1_bias,
    w_up,
    b_up,
    w_down,
    b_down,
    ln2_gain,
    ln2_bias,
):
    groups = lax.axis_size("tensor")
    tensor_rank = lax.axis_index("tensor")
    batches = inputs.shape[1]
    local_rows = inputs.shape[2]
    model_width = inputs.shape[3]
    full_rows = local_rows * groups
    head_width = w_qkv.shape[2]
    flat_qkv = w_qkv.reshape(model_width, 3 * head_width)
    positions = tensor_rank * local_rows + jnp.arange(local_rows, dtype=jnp.int32)
    all_positions = jnp.arange(full_rows, dtype=jnp.int32)
    gain_first = ln1_gain.astype(jnp.float32)
    shift_first = ln1_bias.astype(jnp.float32)

    def micro_batch(batch_index, carried):
        weight_grads, shared_grads, output_rows, input_grads = carried
        tokens = lax.dynamic_index_in_dim(inputs[0], batch_index, 0, keepdims=False)
        incoming = lax.dynamic_index_in_dim(cotangent[0], batch_index, 0, keepdims=False).astype(
            jnp.float32
        )
        length = lax.dynamic_index_in_dim(lengths[0], batch_index, 0, keepdims=False)
        key_mask = all_positions < length
        row_mask = (positions < length).astype(jnp.float32)[:, None]
        tokens_all = lax.all_gather(tokens, "tensor", axis=0, tiled=True)
        projected = jnp.dot(tokens_all, flat_qkv, preferred_element_type=jnp.float32).reshape(
            full_rows, 3, head_width
        )
        queries = (projected[:, 0] + b_query).astype(jnp.bfloat16)
        keys_low = projected[:, 1].astype(jnp.bfloat16)
        values_low = (projected[:, 2] + b_value).astype(jnp.bfloat16)
        context, log_totals = attention_forward(queries, keys_low, values_low, key_mask)
        attended = (
            lax.psum_scatter(
                jnp.dot(context, w_out, preferred_element_type=jnp.float32).astype(jnp.bfloat16),
                "tensor",
                scatter_dimension=0,
                tiled=True,
            ).astype(jnp.float32)
            + b_out
        )
        normed, norm1_back = jax.vjp(
            layer_norm, tokens.astype(jnp.float32) + attended, gain_first, shift_first
        )
        normed_all = lax.all_gather(normed.astype(jnp.bfloat16), "tensor", axis=0, tiled=True)
        hidden = jnp.dot(normed_all, w_up, preferred_element_type=jnp.float32) + b_up
        activated, gelu_back = jax.vjp(exact_gelu, hidden)
        activated_low = activated.astype(jnp.bfloat16)
        mixed = (
            lax.psum_scatter(
                jnp.dot(activated_low, w_down, preferred_element_type=jnp.float32).astype(
                    jnp.bfloat16
                ),
                "tensor",
                scatter_dimension=0,
                tiled=True,
            ).astype(jnp.float32)
            + b_down
        )
        result, norm2_back = jax.vjp(
            layer_norm, normed + mixed, ln2_gain.astype(jnp.float32), ln2_bias.astype(jnp.float32)
        )
        output_rows = lax.dynamic_update_index_in_dim(
            output_rows, (result * row_mask).astype(jnp.bfloat16), batch_index, 0
        )
        grad_second, grad_gain2, grad_shift2 = norm2_back(incoming * row_mask)
        grad_mixed_all = lax.all_gather(
            grad_second.astype(jnp.bfloat16), "tensor", axis=0, tiled=True
        )
        grad_downw = jnp.einsum(
            "sf,sd->fd", activated_low, grad_mixed_all, preferred_element_type=jnp.float32
        )
        grad_activated = jnp.einsum(
            "sd,fd->sf", grad_mixed_all, w_down, preferred_element_type=jnp.float32
        )
        (grad_hidden,) = gelu_back(grad_activated)
        grad_hidden_low = grad_hidden.astype(jnp.bfloat16)
        grad_upw = jnp.einsum(
            "sd,sf->df", normed_all, grad_hidden_low, preferred_element_type=jnp.float32
        )
        acc_qkv, acc_query, acc_value, acc_outw, acc_upw, acc_upb, acc_downw = weight_grads
        acc_upw = acc_upw + grad_upw
        acc_upb = acc_upb + jnp.sum(grad_hidden, axis=0)
        acc_downw = acc_downw + grad_downw
        grad_normed = (
            lax.psum_scatter(
                jnp.einsum(
                    "sf,df->sd", grad_hidden_low, w_up, preferred_element_type=jnp.float32
                ).astype(jnp.bfloat16),
                "tensor",
                scatter_dimension=0,
                tiled=True,
            ).astype(jnp.float32)
            + grad_second
        )
        grad_first, grad_gain1, grad_shift1 = norm1_back(grad_normed)
        grad_attended_all = lax.all_gather(
            grad_first.astype(jnp.bfloat16), "tensor", axis=0, tiled=True
        )
        grad_outw = jnp.einsum(
            "sl,sd->ld", context, grad_attended_all, preferred_element_type=jnp.float32
        )
        grad_context = jnp.einsum(
            "sd,ld->sl", grad_attended_all, w_out, preferred_element_type=jnp.float32
        ).astype(jnp.bfloat16)
        grad_queries, grad_keys, grad_values = attention_backward(
            queries, keys_low, values_low, grad_context, key_mask, log_totals
        )
        grad_projected = (
            jnp.stack([grad_queries, grad_keys, grad_values], axis=1)
            .astype(jnp.bfloat16)
            .reshape(full_rows, 3 * head_width)
        )
        grad_qkvw = jnp.einsum(
            "sd,sk->dk", tokens_all, grad_projected, preferred_element_type=jnp.float32
        ).reshape(model_width, 3, head_width)
        grad_tokens = (
            lax.psum_scatter(
                jnp.einsum(
                    "sk,dk->sd", grad_projected, flat_qkv, preferred_element_type=jnp.float32
                ).astype(jnp.bfloat16),
                "tensor",
                scatter_dimension=0,
                tiled=True,
            ).astype(jnp.float32)
            + grad_first
        )
        input_grads = lax.dynamic_update_index_in_dim(
            input_grads, grad_tokens.astype(jnp.bfloat16), batch_index, 0
        )
        weight_grads = (
            acc_qkv + grad_qkvw,
            acc_query + jnp.sum(grad_queries, axis=0),
            acc_value + jnp.sum(grad_values, axis=0),
            acc_outw + grad_outw,
            acc_upw,
            acc_upb,
            acc_downw,
        )
        shared_outb, shared_gain1, shared_shift1, shared_downb, shared_gain2, shared_shift2 = (
            shared_grads
        )
        shared_grads = (
            shared_outb + jnp.sum(grad_first, axis=0),
            shared_gain1 + grad_gain1,
            shared_shift1 + grad_shift1,
            shared_downb + jnp.sum(grad_second, axis=0),
            shared_gain2 + grad_gain2,
            shared_shift2 + grad_shift2,
        )
        return (weight_grads, shared_grads, output_rows, input_grads)

    vector_zero = jnp.zeros((model_width,), jnp.float32)
    weight_zero = (
        jnp.zeros(w_qkv.shape, jnp.float32),
        jnp.zeros(b_query.shape, jnp.float32),
        jnp.zeros(b_value.shape, jnp.float32),
        jnp.zeros(w_out.shape, jnp.float32),
        jnp.zeros(w_up.shape, jnp.float32),
        jnp.zeros(b_up.shape, jnp.float32),
        jnp.zeros(w_down.shape, jnp.float32),
    )
    shared_zero = (vector_zero, vector_zero, vector_zero, vector_zero, vector_zero, vector_zero)
    rows_zero = jnp.zeros((batches, local_rows, model_width), jnp.bfloat16)
    carried = (weight_zero, shared_zero, rows_zero, rows_zero)
    carried = lax.fori_loop(
        0, batches - 1, lambda batch_index, state_now: micro_batch(batch_index, state_now), carried
    )
    weight_grads, shared_grads, output_rows, input_grads = micro_batch(batches - 1, carried)
    acc_qkv, acc_query, acc_value, acc_outw, acc_upw, acc_upb, acc_downw = weight_grads
    acc_qkv, acc_query, acc_value, acc_outw, acc_upw, acc_upb, acc_downw = lax.psum(
        (acc_qkv, acc_query, acc_value, acc_outw, acc_upw, acc_upb, acc_downw), "dp"
    )
    shared_outb, shared_gain1, shared_shift1, shared_downb, shared_gain2, shared_shift2 = (
        shared_grads
    )
    shared_outb, shared_gain1, shared_shift1, shared_downb, shared_gain2, shared_shift2 = lax.psum(
        (shared_outb, shared_gain1, shared_shift1, shared_downb, shared_gain2, shared_shift2),
        ("dp", "tensor"),
    )
    return (
        output_rows[None],
        input_grads[None],
        acc_qkv,
        acc_query,
        acc_value,
        acc_outw,
        shared_outb,
        shared_gain1,
        shared_shift1,
        acc_upw,
        acc_upb,
        acc_downw,
        shared_downb,
        shared_gain2,
        shared_shift2,
    )


def solution(mesh):
    return jax.shard_map(
        per_device,
        mesh=mesh,
        in_specs=(
            P("dp", None, "tensor", None),
            P("dp", None),
            P("dp", None, "tensor", None),
            P(None, None, "tensor"),
            P("tensor"),
            P("tensor"),
            P("tensor", None),
            P(),
            P(),
            P(),
            P(None, "tensor"),
            P("tensor"),
            P("tensor", None),
            P(),
            P(),
            P(),
        ),
        out_specs=(
            P("dp", None, "tensor", None),
            P("dp", None, "tensor", None),
            P(None, None, "tensor"),
            P("tensor"),
            P("tensor"),
            P("tensor", None),
            P(),
            P(),
            P(),
            P(None, "tensor"),
            P("tensor"),
            P("tensor", None),
            P(),
            P(),
            P(),
        ),
        check_vma=False,
    )
```

profile of v0, /device:TPU:0, one launch (start us, length us, event | category | flops | bytes accessed | tf_op | source)
XLA Modules:
  0.0 1141.6 jit_solution(16924107983350090412)
XLA Ops:
  14.1 15.5 %all-gather.20.cloned.1.call-done = bf16[1,1,512,1024]{3,2,1,0:T(8,128)(2,1)} async-done(((bf16[1,1,128,1024]{3,2,1,0:T(8,128)(2,1)}), bf16[1,1,512,1024]{3,2,1,0:T(8,128)(2,1)}) %all-gather.20.cloned.1.call-update) | async-done | bytes 1048592 | tf_op jit(solution)/shard_map/all_gather | solution.py:154
  39.3 24.9 %reduce-scatter.9.cloned.1.call-done = bf16[128,1024]{1,0:T(8,128)(2,1)} async-done(((bf16[512,1024]{1,0:T(8,128)(2,1)}), bf16[128,1024]{1,0:T(8,128)(2,1)}) %reduce-scatter.9.cloned.1.call-update) | async-done | bytes 262160 | tf_op jit(solution)/shard_map/reduce_scatter | solution.py:163
  68.6 16.8 %all-gather.14.cloned.1.call-done = bf16[512,1024]{1,0:T(8,128)(2,1)} async-done(((bf16[128,1024]{1,0:T(8,128)(2,1)}), bf16[512,1024]{1,0:T(8,128)(2,1)}) %all-gather.14.cloned.1.call-update) | async-done | bytes 1048592 | tf_op jit(solution)/shard_map/all_gather | solution.py:174
  85.5 8.6 multiply_convert_fusion.4
  98.1 24.3 %reduce-scatter.11.cloned.1.call-done = bf16[128,1024]{1,0:T(8,128)(2,1)} async-done(((bf16[512,1024]{1,0:T(8,128)(2,1)}), bf16[128,1024]{1,0:T(8,128)(2,1)}) %reduce-scatter.11.cloned.1.call-update) | async-done | bytes 262160 | tf_op jit(solution)/shard_map/reduce_scatter | solution.py:179
  128.3 16.6 %all-gather.16.cloned.1.call-done = bf16[512,1024]{1,0:T(8,128)(2,1)} async-done(((bf16[128,1024]{1,0:T(8,128)(2,1)}), bf16[512,1024]{1,0:T(8,128)(2,1)}) %all-gather.16.cloned.1.call-update) | async-done | bytes 1048592 | tf_op jit(solution)/shard_map/all_gather | solution.py:196
  154.1 25.0 %reduce-scatter.13.cloned.1.call-done = bf16[128,1024]{1,0:T(8,128)(2,1)} async-done(((bf16[512,1024]{1,0:T(8,128)(2,1)}), bf16[128,1024]{1,0:T(8,128)(2,1)}) %reduce-scatter.13.cloned.1.call-update) | async-done | bytes 262160 | tf_op jit(solution)/shard_map/reduce_scatter | solution.py:215
  186.5 15.1 %all-gather.18.cloned.1.call-done = bf16[512,1024]{1,0:T(8,128)(2,1)} async-done(((bf16[128,1024]{1,0:T(8,128)(2,1)}), bf16[512,1024]{1,0:T(8,128)(2,1)}) %all-gather.18.cloned.1.call-update) | async-done | bytes 1048592 | tf_op jit(solution)/shard_map/all_gather | solution.py:226
  216.0 471.7 %while.48 = (s32[]{:T(128)}, f32[1024,3,256]{2,0,1:T(8,128)}, f32[256]{0:T(256)S(1)}, f32[256]{0:T(256)S(1)}, f32[256,1024]{1,0:T(8,128)}, /*index=5*/f32[1024,1...) while((s32[]{:T(128)}, f32[1024,3,256]{2,0,1:T(8,128)}, ...), condition=%wide.region_25.26_spmd.clone, body=%wide.region_0.25_spmd.clone.sunk | while | flops 10556682240 | bytes 257279664 | solution.py:295
  235.0 16.0 %all-gather.22.cloned.1.call-done = bf16[1,1,512,1024]{3,2,1,0:T(8,128)(2,1)} async-done(((bf16[1,1,128,1024]{3,2,1,0:T(8,128)(2,1)}), bf16[1,1,512,1024]{3,2,1,0:T(8,128)(2,1)}) %all-gather.22.cloned.1.call-update) | async-done | bytes 1048592 | tf_op jit(solution)/shard_map/while/body/eval_jaxpr/all_gather | solution.py:154
  260.5 25.0 %reduce-scatter.17.cloned.1.call-done = bf16[128,1024]{1,0:T(8,128)(2,1)} async-done(((bf16[512,1024]{1,0:T(8,128)(2,1)}), bf16[128,1024]{1,0:T(8,128)(2,1)}) %reduce-scatter.17.cloned.1.call-update) | async-done | bytes 262160 | tf_op jit(solution)/shard_map/while/body/eval_jaxpr/reduce_scatter | solution.py:163
  290.0 16.8 %all-gather.24.cloned.1.call-done = bf16[512,1024]{1,0:T(8,128)(2,1)} async-done(((bf16[128,1024]{1,0:T(8,128)(2,1)}), bf16[512,1024]{1,0:T(8,128)(2,1)}) %all-gather.24.cloned.1.call-update) | async-done | bytes 1048592 | tf_op jit(solution)/shard_map/while/body/eval_jaxpr/all_gather | solution.py:174
  306.8 8.7 multiply_convert_fusion.8
  318.5 24.3 %reduce-scatter.19.cloned.1.call-done = bf16[128,1024]{1,0:T(8,128)(2,1)} async-done(((bf16[512,1024]{1,0:T(8,128)(2,1)}), bf16[128,1024]{1,0:T(8,128)(2,1)}) %reduce-scatter.19.cloned.1.call-update) | async-done | bytes 262160 | tf_op jit(solution)/shard_map/while/body/eval_jaxpr/reduce_scatter | solution.py:179
  347.8 16.8 %all-gather.26.cloned.1.call-done = bf16[512,1024]{1,0:T(8,128)(2,1)} async-done(((bf16[128,1024]{1,0:T(8,128)(2,1)}), bf16[512,1024]{1,0:T(8,128)(2,1)}) %all-gather.26.cloned.1.call-update) | async-done | bytes 1048592 | tf_op jit(solution)/shard_map/while/body/eval_jaxpr/all_gather | solution.py:196
  373.2 25.0 %reduce-scatter.21.cloned.1.call-done = bf16[128,1024]{1,0:T(8,128)(2,1)} async-done(((bf16[512,1024]{1,0:T(8,128)(2,1)}), bf16[128,1024]{1,0:T(8,128)(2,1)}) %reduce-scatter.21.cloned.1.call-update) | async-done | bytes 262160 | tf_op jit(solution)/shard_map/while/body/eval_jaxpr/reduce_scatter | solution.py:215
  408.6 11.0 all-gather.28.cloned.1.call-done
  442.7 15.1 %reduce-scatter.23.cloned.1.call-done = bf16[128,1024]{1,0:T(8,128)(2,1)} async-done(((bf16[512,1024]{1,0:T(8,128)(2,1)}), bf16[128,1024]{1,0:T(8,128)(2,1)}) %reduce-scatter.23.cloned.1.call-update) | async-done | bytes 262160 | tf_op jit(solution)/shard_map/while/body/eval_jaxpr/reduce_scatter | solution.py:247
  463.0 15.7 %all-gather.22.cloned.1.call-done = bf16[1,1,512,1024]{3,2,1,0:T(8,128)(2,1)} async-done(((bf16[1,1,128,1024]{3,2,1,0:T(8,128)(2,1)}), bf16[1,1,512,1024]{3,2,1,0:T(8,128)(2,1)}) %all-gather.22.cloned.1.call-update) | async-done | bytes 1048592 | tf_op jit(solution)/shard_map/while/body/eval_jaxpr/all_gather | solution.py:154
  488.2 25.0 %reduce-scatter.17.cloned.1.call-done = bf16[128,1024]{1,0:T(8,128)(2,1)} async-done(((bf16[512,1024]{1,0:T(8,128)(2,1)}), bf16[128,1024]{1,0:T(8,128)(2,1)}) %reduce-scatter.17.cloned.1.call-update) | async-done | bytes 262160 | tf_op jit(solution)/shard_map/while/body/eval_jaxpr/reduce_scatter | solution.py:163
  517.6 16.8 %all-gather.24.cloned.1.call-done = bf16[512,1024]{1,0:T(8,128)(2,1)} async-done(((bf16[128,1024]{1,0:T(8,128)(2,1)}), bf16[512,1024]{1,0:T(8,128)(2,1)}) %all-gather.24.cloned.1.call-update) | async-done | bytes 1048592 | tf_op jit(solution)/shard_map/while/body/eval_jaxpr/all_gather | solution.py:174
  534.4 8.7 multiply_convert_fusion.8
  546.1 24.3 %reduce-scatter.19.cloned.1.call-done = bf16[128,1024]{1,0:T(8,128)(2,1)} async-done(((bf16[512,1024]{1,0:T(8,128)(2,1)}), bf16[128,1024]{1,0:T(8,128)(2,1)}) %reduce-scatter.19.cloned.1.call-update) | async-done | bytes 262160 | tf_op jit(solution)/shard_map/while/body/eval_jaxpr/reduce_scatter | solution.py:179
  575.5 16.8 %all-gather.26.cloned.1.call-done = bf16[512,1024]{1,0:T(8,128)(2,1)} async-done(((bf16[128,1024]{1,0:T(8,128)(2,1)}), bf16[512,1024]{1,0:T(8,128)(2,1)}) %all-gather.26.cloned.1.call-update) | async-done | bytes 1048592 | tf_op jit(solution)/shard_map/while/body/eval_jaxpr/all_gather | solution.py:196
  600.9 25.0 %reduce-scatter.21.cloned.1.call-done = bf16[128,1024]{1,0:T(8,128)(2,1)} async-done(((bf16[512,1024]{1,0:T(8,128)(2,1)}), bf16[128,1024]{1,0:T(8,128)(2,1)}) %reduce-scatter.21.cloned.1.call-update) | async-done | bytes 262160 | tf_op jit(solution)/shard_map/while/body/eval_jaxpr/reduce_scatter | solution.py:215
  631.4 6.1 select_add_fusion.22
  637.5 9.7 all-gather.28.cloned.1.call-done
  672.8 12.7 %reduce-scatter.23.cloned.1.call-done = bf16[128,1024]{1,0:T(8,128)(2,1)} async-done(((bf16[512,1024]{1,0:T(8,128)(2,1)}), bf16[128,1024]{1,0:T(8,128)(2,1)}) %reduce-scatter.23.cloned.1.call-update) | async-done | bytes 262160 | tf_op jit(solution)/shard_map/while/body/eval_jaxpr/reduce_scatter | solution.py:247
  689.0 6.0 convolution_add_fusion.1
  713.7 43.6 %all-reduce = (f32[1024]{0:T(1024)}, f32[1024]{0:T(1024)}, f32[1024]{0:T(1024)}, f32[1024]{0:T(1024)}, f32[1024]{0:T(1024)}, /*index=5*/f32[1024]{0:T(1024)}) all-reduce(f32[1024]{0:T(1024)S(1)} %add.586, f32[1024]{0:T(1024)S(1)} %add.587, f32[1024]{0:T(1024)S(1)} %add.588, ...), channel_id=1, replica_groups=mesh['dp'=8,'tensor'=4] {'dp','tensor'}, use_global_device_ids=true, to_apply=%region_48.49 | all-reduce | flops 6144 | bytes 49152 | tf_op jit(solution)/shard_map/psum | solution.py:306
  757.4 22.7 %all-reduce.1 = (f32[256]{0:T(256)}, f32[256]{0:T(256)}, f32[1024]{0:T(1024)}) all-reduce(f32[256]{0:T(256)S(1)} %add.583, f32[256]{0:T(256)S(1)} %add.584, f32[1024]{0:T(1024)S(1)} %add.590), channel_id=1, replica_groups=mesh['dp'=8,'tensor'=4] {'dp'}, use_global_device_ids=true, to_apply=%region_43.44 | all-reduce | flops 1536 | bytes 12288 | tf_op jit(solution)/shard_map/psum | solution.py:300
  782.0 342.1 %all-reduce.5.cloned.1.call-done = (f32[1024,3,256]{2,0,1:T(8,128)}, f32[256,1024]{1,0:T(8,128)}, f32[1024,1024]{1,0:T(8,128)}, f32[1024,1024]{1,0:T(8,128)}) async-done(((f32[1024,3,256]{2,0,1:T(8,128)}, f32[256,1024]{1,0:T(8,128)}, f32[1024,1024]{1,0:T(8,128)}, f32[1024,1024]{1,0:T(8,128)}), (f32[1024,3,256]{2,0,1:T(8,128)}, f32[256,1024]{1,0:T(8,128)}, f32[1024,1024]{1,0:T(8,128)}, ...) | async-done | bytes 12582928 | tf_op jit(solution)/shard_map/psum | solution.py:300
  (460 shorter events, 228.6 us)
Async XLA Ops:
  7.2 22.4 %all-gather.20.cloned.1.call-start = ((), (), s32[]{:S(2)}) async-start(), calls=%async_computation.15 | async-start | bytes 1310720 | tf_op jit(solution)/shard_map/all_gather | solution.py:154
  8.9 55.3 %reduce-scatter.9.cloned.1.call-start = ((), (), s32[]{:S(2)}) async-start(), calls=%async_computation.8 | async-start | bytes 1310720 | tf_op jit(solution)/shard_map/reduce_scatter | solution.py:163
  36.6 32.0 %copy-start.46 = (bf16[1024]{0:T(1024)(128)(2,1)S(1)}, bf16[1024]{0:T(1024)(128)(2,1)}, u32[]{:S(2)}) copy-start(bf16[1024]{0:T(1024)(128)(2,1)} %param.29) | copy-start | bytes 6148
  39.2 46.3 %all-gather.14.cloned.1.call-start = ((), (), s32[]{:S(2)}) async-start(), calls=%async_computation.9 | async-start | bytes 1310720 | tf_op jit(solution)/shard_map/all_gather | solution.py:174
  68.6 53.8 %reduce-scatter.11.cloned.1.call-start = ((), (), s32[]{:S(2)}) async-start(), calls=%async_computation.10 | async-start | bytes 1310720 | tf_op jit(solution)/shard_map/reduce_scatter | solution.py:179
  97.3 47.5 %all-gather.16.cloned.1.call-start = ((), (), s32[]{:S(2)}) async-start(), calls=%async_computation.11 | async-start | bytes 1310720 | tf_op jit(solution)/shard_map/all_gather | solution.py:196
  128.0 51.1 %reduce-scatter.13.cloned.1.call-start = ((), (), s32[]{:S(2)}) async-start(), calls=%async_computation.12 | async-start | bytes 1310720 | tf_op jit(solution)/shard_map/reduce_scatter | solution.py:215
  154.0 47.6 %all-gather.18.cloned.1.call-start = ((), (), s32[]{:S(2)}) async-start(), calls=%async_computation.13 | async-start | bytes 1310720 | tf_op jit(solution)/shard_map/all_gather | solution.py:226
  231.8 19.3 %all-gather.22.cloned.1.call-start = ((), (), s32[]{:S(2)}) async-start(), calls=%async_computation.17 | async-start | bytes 1310720 | tf_op jit(solution)/shard_map/while/body/eval_jaxpr/all_gather | solution.py:154
  233.5 52.0 %reduce-scatter.17.cloned.1.call-start = ((), (), s32[]{:S(2)}) async-start(), calls=%async_computation.18 | async-start | bytes 1310720 | tf_op jit(solution)/shard_map/while/body/eval_jaxpr/reduce_scatter | solution.py:163
  257.9 32.0 %copy-start.18 = (bf16[4,64,512]{2,1,0:T(8,128)(2,1)}, bf16[4,64,512]{2,1,0:T(8,128)(2,1)S(1)}, u32[]{:S(2)}) copy-start(bf16[4,64,512]{2,1,0:T(8,128)(2,1)S(1)} %fusion.236) | copy-start | bytes 786436 | tf_op jit(solution)/shard_map/while
  260.5 46.3 %all-gather.24.cloned.1.call-start = ((), (), s32[]{:S(2)}) async-start(), calls=%async_computation.19 | async-start | bytes 1310720 | tf_op jit(solution)/shard_map/while/body/eval_jaxpr/all_gather | solution.py:174
  289.9 52.9 %reduce-scatter.19.cloned.1.call-start = ((), (), s32[]{:S(2)}) async-start(), calls=%async_computation.20 | async-start | bytes 1310720 | tf_op jit(solution)/shard_map/while/body/eval_jaxpr/reduce_scatter | solution.py:179
  317.7 46.9 %all-gather.26.cloned.1.call-start = ((), (), s32[]{:S(2)}) async-start(), calls=%async_computation.21 | async-start | bytes 1310720 | tf_op jit(solution)/shard_map/while/body/eval_jaxpr/all_gather | solution.py:196
  347.7 50.5 %reduce-scatter.21.cloned.1.call-start = ((), (), s32[]{:S(2)}) async-start(), calls=%async_computation.22 | async-start | bytes 1310720 | tf_op jit(solution)/shard_map/while/body/eval_jaxpr/reduce_scatter | solution.py:215
  373.2 46.4 %all-gather.28.cloned.1.call-start = ((), (), s32[]{:S(2)}) async-start(), calls=%async_computation.23 | async-start | bytes 1310720 | tf_op jit(solution)/shard_map/while/body/eval_jaxpr/all_gather | solution.py:226
  402.7 55.1 %reduce-scatter.23.cloned.1.call-start = ((), (), s32[]{:S(2)}) async-start(), calls=%async_computation.24 | async-start | bytes 1310720 | tf_op jit(solution)/shard_map/while/body/eval_jaxpr/reduce_scatter | solution.py:247
  459.8 18.9 %all-gather.22.cloned.1.call-start = ((), (), s32[]{:S(2)}) async-start(), calls=%async_computation.17 | async-start | bytes 1310720 | tf_op jit(solution)/shard_map/while/body/eval_jaxpr/all_gather | solution.py:154
  461.5 51.7 %reduce-scatter.17.cloned.1.call-start = ((), (), s32[]{:S(2)}) async-start(), calls=%async_computation.18 | async-start | bytes 1310720 | tf_op jit(solution)/shard_map/while/body/eval_jaxpr/reduce_scatter | solution.py:163
  485.5 32.0 %copy-start.18 = (bf16[4,64,512]{2,1,0:T(8,128)(2,1)}, bf16[4,64,512]{2,1,0:T(8,128)(2,1)S(1)}, u32[]{:S(2)}) copy-start(bf16[4,64,512]{2,1,0:T(8,128)(2,1)S(1)} %fusion.236) | copy-start | bytes 786436 | tf_op jit(solution)/shard_map/while
  488.1 46.3 %all-gather.24.cloned.1.call-start = ((), (), s32[]{:S(2)}) async-start(), calls=%async_computation.19 | async-start | bytes 1310720 | tf_op jit(solution)/shard_map/while/body/eval_jaxpr/all_gather | solution.py:174
  517.6 52.9 %reduce-scatter.19.cloned.1.call-start = ((), (), s32[]{:S(2)}) async-start(), calls=%async_computation.20 | async-start | bytes 1310720 | tf_op jit(solution)/shard_map/while/body/eval_jaxpr/reduce_scatter | solution.py:179
  545.4 46.9 %all-gather.26.cloned.1.call-start = ((), (), s32[]{:S(2)}) async-start(), calls=%async_computation.21 | async-start | bytes 1310720 | tf_op jit(solution)/shard_map/while/body/eval_jaxpr/all_gather | solution.py:196
  575.4 50.5 %reduce-scatter.21.cloned.1.call-start = ((), (), s32[]{:S(2)}) async-start(), calls=%async_computation.22 | async-start | bytes 1310720 | tf_op jit(solution)/shard_map/while/body/eval_jaxpr/reduce_scatter | solution.py:215
  600.9 46.4 %all-gather.28.cloned.1.call-start = ((), (), s32[]{:S(2)}) async-start(), calls=%async_computation.23 | async-start | bytes 1310720 | tf_op jit(solution)/shard_map/while/body/eval_jaxpr/all_gather | solution.py:226
  630.4 55.2 %reduce-scatter.23.cloned.1.call-start = ((), (), s32[]{:S(2)}) async-start(), calls=%async_computation.24 | async-start | bytes 1310720 | tf_op jit(solution)/shard_map/while/body/eval_jaxpr/reduce_scatter | solution.py:247
  687.7 92.5 %reduce-scatter.15.cloned.1.call-start = ((), (), s32[]{:S(2)}) async-start(), calls=%async_computation.14 | async-start | bytes 1310720 | tf_op jit(solution)/shard_map/reduce_scatter | solution.py:247
  688.3 435.7 %all-reduce.5.cloned.1.call-start = ((), (), s32[]{:S(2)}) async-start(), calls=%async_computation.16 | async-start | bytes 25165824 | tf_op jit(solution)/shard_map/psum | solution.py:300
  711.7 45.6 %copy-start.62 = (f32[4,64]{1,0:T(4,128)S(1)}, f32[4,64]{1,0:T(4,128)}, u32[]{:S(2)}) copy-start(f32[4,64]{1,0:T(4,128)} %get-tuple-element.996) | copy-start | bytes 3076
  711.7 45.6 %copy-start.65 = (f32[4,64]{1,0:T(4,128)S(1)}, f32[4,64]{1,0:T(4,128)}, u32[]{:S(2)}) copy-start(f32[4,64]{1,0:T(4,128)} %get-tuple-element.994) | copy-start | bytes 3076
  711.7 68.4 %copy-start.23 = (f32[128,1024]{1,0:T(8,128)S(1)}, f32[128,1024]{1,0:T(8,128)}, u32[]{:S(2)}) copy-start(f32[128,1024]{1,0:T(8,128)} %copy-done.22) | copy-start | bytes 1572868
  711.8 68.4 %copy-start.74 = (f32[128]{0:T(128)S(1)}, f32[128]{0:T(128)}, u32[]{:S(2)}) copy-start(f32[128]{0:T(128)} %copy-done.73) | copy-start | bytes 1540
  (89 other events, 466.2 us)
Sparse Core Ops, SparseCore 0:
  10.1 19.4 all-gather.19
  39.3 24.8 reduce-scatter.8
  68.7 16.7 all-gather.13
  97.5 24.8 reduce-scatter.10
  128.1 16.7 all-gather.15
  154.1 24.8 reduce-scatter.12
  184.8 16.7 all-gather.17
  234.3 16.7 all-gather.21
  260.6 24.8 reduce-scatter.16
  290.0 16.7 all-gather.23
  317.9 24.8 reduce-scatter.18
  347.8 16.7 all-gather.25
  373.3 24.8 reduce-scatter.20
  402.8 16.7 all-gather.27
  432.9 24.8 reduce-scatter.22
  461.9 16.7 all-gather.21
  488.2 24.8 reduce-scatter.16
  517.7 16.7 all-gather.23
  545.5 24.8 reduce-scatter.18
  575.5 16.7 all-gather.25
  601.0 24.8 reduce-scatter.20
  630.5 16.6 all-gather.27
  660.6 24.9 reduce-scatter.22
  690.9 24.8 reduce-scatter.14
  721.8 402.2 all-reduce.4
where the time goes:
time: 1150 us; the launch traced here: 1140 us
  waiting for transfers between devices  778 us (68%)
  matrix products  156 us (14%)
  blocking collectives  66.3 us (6%)
  other arithmetic  62.9 us (5%)
  local copies, waits for them, and re-layouts  45.9 us (4%)
  loops' own time  16.8 us (1%)
  between operations  15.1 us (1%)
    psum x1, waiting for transfers between devices, per_device(): lax.psum((acc_qkv, acc_query, acc_value, acc_outw, acc_upw, acc_upb, acc_...  342 us
    reduce_scatter x3, waiting for transfers between devices, micro_batch(): lax.psum_scatter(jnp.einsum('sf,df->sd', grad_hidden_low, w_up, preferred...  75 us
    reduce_scatter x3, waiting for transfers between devices, micro_batch(): lax.psum_scatter(jnp.dot(context, w_out, preferred_element_type=jnp.float...  74.9 us
    reduce_scatter x3, waiting for transfers between devices, micro_batch(): lax.psum_scatter(jnp.dot(activated_low, w_down, preferred_element_type=jn...  72.9 us
    all_gather x3, waiting for transfers between devices, micro_batch(): lax.all_gather(normed.astype(jnp.bfloat16), 'tensor', axis=0, tiled=True)  50.4 us
    all_gather x3, waiting for transfers between devices, micro_batch(): lax.all_gather(grad_second.astype(jnp.bfloat16), 'tensor', axis=0, tiled=...  50.2 us
    all_gather x3, waiting for transfers between devices, micro_batch(): tokens_all = lax.all_gather(tokens, 'tensor', axis=0, tiled=True)  47.3 us
    psum x1, blocking collectives, per_device(): lax.psum((shared_outb, shared_gain1, shared_shift1, shared_downb, shared_...  43.6 us
  transfers between devices with their start and end apart: 25, of which 24 were waited for; matrix products, arithmetic and copies ran while one was open for 6% of the time, Pallas kernels for 0%

commit v1 on v0

--- a/solution.py
+++ b/solution.py
@@ -292,14 +292,15 @@
     shared_zero = (vector_zero, vector_zero, vector_zero, vector_zero, vector_zero, vector_zero)
     rows_zero = jnp.zeros((batches, local_rows, model_width), jnp.bfloat16)
     carried = (weight_zero, shared_zero, rows_zero, rows_zero)
-    carried = lax.fori_loop(
-        0, batches - 1, lambda batch_index, state_now: micro_batch(batch_index, state_now), carried
-    )
+    for batch_index in range(batches - 1):
+        carried = micro_batch(batch_index, carried)
     weight_grads, shared_grads, output_rows, input_grads = micro_batch(batches - 1, carried)
     acc_qkv, acc_query, acc_value, acc_outw, acc_upw, acc_upb, acc_downw = weight_grads
-    acc_qkv, acc_query, acc_value, acc_outw, acc_upw, acc_upb, acc_downw = lax.psum(
-        (acc_qkv, acc_query, acc_value, acc_outw, acc_upw, acc_upb, acc_downw), "dp"
-    )
+    acc_qkv, acc_outw, acc_upw, acc_downw = (
+        lax.psum(term.astype(jnp.bfloat16), "dp").astype(jnp.float32)
+        for term in (acc_qkv, acc_outw, acc_upw, acc_downw)
+    )
+    acc_query, acc_value, acc_upb = lax.psum((acc_query, acc_value, acc_upb), "dp")
     shared_outb, shared_gain1, shared_shift1, shared_downb, shared_gain2, shared_shift2 = (
         shared_grads
     )

time: 1150 us -> 857 us (0.75)
  waiting for transfers between devices: 778 us -> 487 us
  loops' own time: 16.8 us -> 0 us
    psum x1, waiting for transfers between devices: 342 us -> 169 us  [per_device(): lax.psum(term.astype(jnp.bfloat16), 'dp').astype(jnp.float32)]
    all_gather x3, waiting for transfers between devices: 35.9 us -> 3.15 us  [micro_batch(): lax.all_gather(grad_first.astype(jnp.bfloat16), 'tensor', axis=0, tiled=T...]
    reduce_scatter x3, waiting for transfers between devices: 27.9 us -> 0.04 us  [micro_batch(): lax.psum_scatter(jnp.einsum('sk,dk->sd', grad_projected, flat_qkv, prefer...]
    reduce_scatter x3, waiting for transfers between devices: 75 us -> 52.3 us  [micro_batch(): lax.psum_scatter(jnp.einsum('sf,df->sd', grad_hidden_low, w_up, preferred...]
    another operation x1 -> x0, loops' own time: 16.8 us -> none  [per_device(): lax.fori_loop(0, batches - 1, lambda batch_index, state_now: micro_batch(...]
    all_gather x3, waiting for transfers between devices: 47.3 us -> 32.8 us  [micro_batch(): tokens_all = lax.all_gather(tokens, 'tensor', axis=0, tiled=True)]
    all_gather x3, waiting for transfers between devices: 50.2 us -> 37.4 us  [micro_batch(): lax.all_gather(grad_second.astype(jnp.bfloat16), 'tensor', axis=0, tiled=...]
    another operation x3 -> x9, local copies, waits for them, and re-layouts: 0.4 us -> 12.6 us  [micro_batch(): jnp.stack([grad_queries, grad_keys, grad_values], axis=1)]
  transfers between devices with their start and end apart: 25 -> 25, of which waited for: 24 -> 20; matrix products, arithmetic and copies ran while one was open for 6% -> 23% of each run, Pallas kernels for 0% -> 0%
where the time goes in v1:
time: 857 us; the launch traced here: 849 us
  waiting for transfers between devices  487 us (57%)
  matrix products  162 us (19%)
  other arithmetic  69.7 us (8%)
  blocking collectives  64.5 us (8%)
  local copies, waits for them, and re-layouts  47.5 us (6%)
  between operations  16.1 us (2%)
    psum x1, waiting for transfers between devices, per_device(): lax.psum(term.astype(jnp.bfloat16), 'dp').astype(jnp.float32)  169 us
    reduce_scatter x3, waiting for transfers between devices, micro_batch(): lax.psum_scatter(jnp.dot(context, w_out, preferred_element_type=jnp.float...  73.4 us
    reduce_scatter x3, waiting for transfers between devices, micro_batch(): lax.psum_scatter(jnp.dot(activated_low, w_down, preferred_element_type=jn...  67.9 us
    reduce_scatter x3, waiting for transfers between devices, micro_batch(): lax.psum_scatter(jnp.einsum('sf,df->sd', grad_hidden_low, w_up, preferred...  52.3 us
    all_gather x3, waiting for transfers between devices, micro_batch(): lax.all_gather(normed.astype(jnp.bfloat16), 'tensor', axis=0, tiled=True)  47.9 us
    psum x1, blocking collectives, per_device(): lax.psum((shared_outb, shared_gain1, shared_shift1, shared_downb, shared_...  40.6 us
    all_gather x3, waiting for transfers between devices, micro_batch(): lax.all_gather(grad_second.astype(jnp.bfloat16), 'tensor', axis=0, tiled=...  37.4 us
    all_gather x3, waiting for transfers between devices, micro_batch(): tokens_all = lax.all_gather(tokens, 'tensor', axis=0, tiled=True)  32.8 us
  transfers between devices with their start and end apart: 25, of which 20 were waited for; matrix products, arithmetic and copies ran while one was open for 23% of the time, Pallas kernels for 0%

profile of v1, /device:TPU:0, one launch (start us, length us, event | category | flops | bytes accessed | tf_op | source)
XLA Modules:
  0.0 848.8 jit_solution(5004472759297793893)
XLA Ops:
  16.3 13.4 %all-gather.38.cloned.1.call-done = bf16[1,1,512,1024]{3,2,1,0:T(8,128)(2,1)} async-done(((bf16[1,1,128,1024]{3,2,1,0:T(8,128)(2,1)}), bf16[1,1,512,1024]{3,2,1,0:T(8,128)(2,1)}) %all-gather.38.cloned.1.call-update) | async-done | bytes 1048592 | tf_op jit(solution)/shard_map/all_gather | solution.py:154
  38.7 9.8 %all-gather.34.cloned.1.call-done = bf16[1,1,512,1024]{3,2,1,0:T(8,128)(2,1)} async-done(((bf16[1,1,128,1024]{3,2,1,0:T(8,128)(2,1)}), bf16[1,1,512,1024]{3,2,1,0:T(8,128)(2,1)}) %all-gather.34.cloned.1.call-update) | async-done | bytes 1048592 | tf_op jit(solution)/shard_map/all_gather | solution.py:154
  57.9 9.6 %all-gather.36.cloned.1.call-done = bf16[1,1,512,1024]{3,2,1,0:T(8,128)(2,1)} async-done(((bf16[1,1,128,1024]{3,2,1,0:T(8,128)(2,1)}), bf16[1,1,512,1024]{3,2,1,0:T(8,128)(2,1)}) %all-gather.36.cloned.1.call-update) | async-done | bytes 1048592 | tf_op jit(solution)/shard_map/all_gather | solution.py:154
  76.6 18.8 %reduce-scatter.21.cloned.1.call-done = bf16[128,1024]{1,0:T(8,128)(2,1)} async-done(((bf16[512,1024]{1,0:T(8,128)(2,1)}), bf16[128,1024]{1,0:T(8,128)(2,1)}) %reduce-scatter.21.cloned.1.call-update) | async-done | bytes 262160 | tf_op jit(solution)/shard_map/reduce_scatter | solution.py:163
  95.4 28.0 %reduce-scatter.13.cloned.1.call-done = bf16[128,1024]{1,0:T(8,128)(2,1)} async-done(((bf16[512,1024]{1,0:T(8,128)(2,1)}), bf16[128,1024]{1,0:T(8,128)(2,1)}) %reduce-scatter.13.cloned.1.call-update) | async-done | bytes 262160 | tf_op jit(solution)/shard_map/reduce_scatter | solution.py:163
  124.7 26.6 %reduce-scatter.17.cloned.1.call-done = bf16[128,1024]{1,0:T(8,128)(2,1)} async-done(((bf16[512,1024]{1,0:T(8,128)(2,1)}), bf16[128,1024]{1,0:T(8,128)(2,1)}) %reduce-scatter.17.cloned.1.call-update) | async-done | bytes 262160 | tf_op jit(solution)/shard_map/reduce_scatter | solution.py:163
  156.0 16.1 %all-gather.18.cloned.1.call-done = bf16[512,1024]{1,0:T(8,128)(2,1)} async-done(((bf16[128,1024]{1,0:T(8,128)(2,1)}), bf16[512,1024]{1,0:T(8,128)(2,1)}) %all-gather.18.cloned.1.call-update) | async-done | bytes 1048592 | tf_op jit(solution)/shard_map/all_gather | solution.py:174
  175.9 15.2 %all-gather.20.cloned.1.call-done = bf16[512,1024]{1,0:T(8,128)(2,1)} async-done(((bf16[128,1024]{1,0:T(8,128)(2,1)}), bf16[512,1024]{1,0:T(8,128)(2,1)}) %all-gather.20.cloned.1.call-update) | async-done | bytes 1048592 | tf_op jit(solution)/shard_map/all_gather | solution.py:174
  191.1 13.0 %multiply_convert_fusion.3 = (bf16[512,1024]{1,0:T(8,128)(2,1)S(1)}, f32[512,1024]{1,0:T(8,128)}, bf16[512,1024]{1,0:T(8,128)(2,1)}, f32[512,1024]{1,0:T(8,128)}, f32[512,1024]{1,0:T(8,128)}) fusion(f32[1024]{0:T(1024)S(1)} %convert_element_type.389, f32[512,1024]{1,0:T(8,128)} %fusion.137, bf16[512,1024]{1,0:T(8,128)(2,1)} %all-gather.20.cloned.1.call-done, ...), kind=kOutput, calls=%fused_computation.45 | convolution fusion | flops 1142947840 | bytes 13635584 | tf_op jit(solution)/shard_map/dot_general | solution.py:175
  211.8 20.7 %reduce-scatter.23.cloned.1.call-done = bf16[128,1024]{1,0:T(8,128)(2,1)} async-done(((bf16[512,1024]{1,0:T(8,128)(2,1)}), bf16[128,1024]{1,0:T(8,128)(2,1)}) %reduce-scatter.23.cloned.1.call-update) | async-done | bytes 262160 | tf_op jit(solution)/shard_map/reduce_scatter | solution.py:179
  232.5 27.3 %reduce-scatter.19.cloned.1.call-done = bf16[128,1024]{1,0:T(8,128)(2,1)} async-done(((bf16[512,1024]{1,0:T(8,128)(2,1)}), bf16[128,1024]{1,0:T(8,128)(2,1)}) %reduce-scatter.19.cloned.1.call-update) | async-done | bytes 262160 | tf_op jit(solution)/shard_map/reduce_scatter | solution.py:179
  262.7 16.6 %all-gather.16.cloned.1.call-done = bf16[512,1024]{1,0:T(8,128)(2,1)} async-done(((bf16[128,1024]{1,0:T(8,128)(2,1)}), bf16[512,1024]{1,0:T(8,128)(2,1)}) %all-gather.16.cloned.1.call-update) | async-done | bytes 1048592 | tf_op jit(solution)/shard_map/all_gather | solution.py:174
  279.3 8.4 multiply_convert_fusion.5
  296.1 20.0 %reduce-scatter.15.cloned.1.call-done = bf16[128,1024]{1,0:T(8,128)(2,1)} async-done(((bf16[512,1024]{1,0:T(8,128)(2,1)}), bf16[128,1024]{1,0:T(8,128)(2,1)}) %reduce-scatter.15.cloned.1.call-update) | async-done | bytes 262160 | tf_op jit(solution)/shard_map/reduce_scatter | solution.py:179
  330.1 10.1 %all-gather.22.cloned.1.call-done = bf16[512,1024]{1,0:T(8,128)(2,1)} async-done(((bf16[128,1024]{1,0:T(8,128)(2,1)}), bf16[512,1024]{1,0:T(8,128)(2,1)}) %all-gather.22.cloned.1.call-update) | async-done | bytes 1048592 | tf_op jit(solution)/shard_map/all_gather | solution.py:196
  340.2 4.5 fusion.138
  344.8 13.6 %all-gather.30.cloned.1.call-done = bf16[512,1024]{1,0:T(8,128)(2,1)} async-done(((bf16[128,1024]{1,0:T(8,128)(2,1)}), bf16[512,1024]{1,0:T(8,128)(2,1)}) %all-gather.30.cloned.1.call-update) | async-done | bytes 1048592 | tf_op jit(solution)/shard_map/all_gather | solution.py:196
  358.4 4.5 fusion.139
  362.9 13.6 %all-gather.26.cloned.1.call-done = bf16[512,1024]{1,0:T(8,128)(2,1)} async-done(((bf16[128,1024]{1,0:T(8,128)(2,1)}), bf16[512,1024]{1,0:T(8,128)(2,1)}) %all-gather.26.cloned.1.call-update) | async-done | bytes 1048592 | tf_op jit(solution)/shard_map/all_gather | solution.py:196
  376.6 12.2 %fusion.114 = (f32[1024]{0:T(1024)}, bf16[512,1024]{1,0:T(8,128)(2,1)}, f32[1024]{0:T(1024)}, bf16[512,1024]{1,0:T(8,128)(2,1)S(1)}, f32[1024]{0:T(1024)}, /*index=5*/bf16[512,1024]{1,0:T(8,128)(2,1)}) fusion(f32[512,1024]{1,0:T(8,128)} %get-tuple-element.279, f32[512,1024]{1,0:T(8,128)} %fusion.137, f32[1024]{0:T(1024)S(1)} %copy-done.94, ...), kind=kOutput, calls=%fused_computation.302 | convolution fusion | flops 1098904576 | bytes 23085056 | tf_op jit(solution)/shard_map/sd,fd->sf/dot_general | solution.py:202
  399.5 5.0 fusion.80
  407.9 9.3 %reduce-scatter.25.cloned.1.call-done = bf16[128,1024]{1,0:T(8,128)(2,1)} async-done(((bf16[512,1024]{1,0:T(8,128)(2,1)}), bf16[128,1024]{1,0:T(8,128)(2,1)}) %reduce-scatter.25.cloned.1.call-update) | async-done | bytes 262160 | tf_op jit(solution)/shard_map/reduce_scatter | solution.py:215
  422.1 6.9 add_convert_fusion.1
  428.9 15.7 %reduce-scatter.33.cloned.1.call-done = bf16[128,1024]{1,0:T(8,128)(2,1)} async-done(((bf16[512,1024]{1,0:T(8,128)(2,1)}), bf16[128,1024]{1,0:T(8,128)(2,1)}) %reduce-scatter.33.cloned.1.call-update) | async-done | bytes 262160 | tf_op jit(solution)/shard_map/reduce_scatter | solution.py:215
  444.6 27.3 %reduce-scatter.29.cloned.1.call-done = bf16[128,1024]{1,0:T(8,128)(2,1)} async-done(((bf16[512,1024]{1,0:T(8,128)(2,1)}), bf16[128,1024]{1,0:T(8,128)(2,1)}) %reduce-scatter.29.cloned.1.call-update) | async-done | bytes 262160 | tf_op jit(solution)/shard_map/reduce_scatter | solution.py:215
  492.7 5.3 multiply_reduce_fusion.2
  501.4 4.7 multiply_convert_fusion.2
  520.0 5.3 multiply_reduce_fusion.1
  528.6 4.7 multiply_convert_fusion.1
  594.2 40.6 %all-reduce.2 = (f32[1024]{0:T(1024)}, f32[1024]{0:T(1024)}, f32[1024]{0:T(1024)}, f32[1024]{0:T(1024)}, f32[1024]{0:T(1024)}, /*index=5*/f32[1024]{0:T(1024)}) all-reduce(f32[1024]{0:T(1024)S(1)} %add_add_fusion.15, f32[1024]{0:T(1024)S(1)} %add_add_fusion.14, ...), channel_id=1, replica_groups=mesh['dp'=8,'tensor'=4] {'dp','tensor'}, use_global_device_ids=true, to_apply=%region_58.59 | all-reduce | flops 6144 | bytes 49152 | tf_op jit(solution)/shard_map/psum | solution.py:307
  635.1 23.9 %all-reduce.3 = (f32[256]{0:T(256)}, f32[256]{0:T(256)}, f32[1024]{0:T(1024)}) all-reduce(f32[256]{0:T(256)S(1)} %add.523, f32[256]{0:T(256)S(1)} %add.526, f32[1024]{0:T(1024)S(1)} %add_add_fusion.12), channel_id=1, replica_groups=mesh['dp'=8,'tensor'=4] {'dp'}, use_global_device_ids=true, to_apply=%region_49.50 | all-reduce | flops 1536 | bytes 12288 | tf_op jit(solution)/shard_map/psum | solution.py:303
  662.8 169.5 %all-reduce.7.cloned.1.call-done = (bf16[1024,3,256]{2,0,1:T(8,128)(2,1)}, bf16[256,1024]{1,0:T(8,128)(2,1)}, bf16[1024,1024]{1,0:T(8,128)(2,1)}, bf16[1024,1024]{1,0:T(8,128)(2,1)}) async-done(((bf16[1024,3,256]{2,0,1:T(8,128)(2,1)}, bf16[256,1024]{1,0:T(8,128)(2,1)}, bf16[1024,1024]{1,0:T(8,128)(2,1)}, bf16[1024,1024]{1,0:T(8,128)(2,1)}), (bf16[1024,3,256]{2,0,1:T(8,128)(2,1)}, ...) | async-done | bytes 6291472 | tf_op jit(solution)/shard_map/psum | solution.py:300
  (456 shorter events, 212.5 us)
Async XLA Ops:
  7.2 164.9 %copy-start = (bf16[1024,1024]{1,0:T(8,128)(2,1)S(1)}, bf16[1024,1024]{1,0:T(8,128)(2,1)}, u32[]{:S(2)}) copy-start(bf16[1024,1024]{1,0:T(8,128)(2,1)} %param.26) | copy-start | bytes 6291460
  7.2 22.4 %all-gather.38.cloned.1.call-start = ((), (), s32[]{:S(2)}) async-start(), calls=%async_computation.35 | async-start | bytes 1310720 | tf_op jit(solution)/shard_map/all_gather | solution.py:154
  9.4 39.1 %all-gather.34.cloned.1.call-start = ((), (), s32[]{:S(2)}) async-start(), calls=%async_computation.33 | async-start | bytes 1310720 | tf_op jit(solution)/shard_map/all_gather | solution.py:154
  10.2 57.3 %all-gather.36.cloned.1.call-start = ((), (), s32[]{:S(2)}) async-start(), calls=%async_computation.34 | async-start | bytes 1310720 | tf_op jit(solution)/shard_map/all_gather | solution.py:154
  10.9 84.5 %reduce-scatter.21.cloned.1.call-start = ((), (), s32[]{:S(2)}) async-start(), calls=%async_computation.18 | async-start | bytes 1310720 | tf_op jit(solution)/shard_map/reduce_scatter | solution.py:163
  38.7 84.7 %reduce-scatter.13.cloned.1.call-start = ((), (), s32[]{:S(2)}) async-start(), calls=%async_computation.12 | async-start | bytes 1310720 | tf_op jit(solution)/shard_map/reduce_scatter | solution.py:163
  57.6 93.7 %reduce-scatter.17.cloned.1.call-start = ((), (), s32[]{:S(2)}) async-start(), calls=%async_computation.15 | async-start | bytes 1310720 | tf_op jit(solution)/shard_map/reduce_scatter | solution.py:163
  76.5 95.6 %all-gather.18.cloned.1.call-start = ((), (), s32[]{:S(2)}) async-start(), calls=%async_computation.16 | async-start | bytes 1310720 | tf_op jit(solution)/shard_map/all_gather | solution.py:174
  95.4 58.7 %copy-start.13 = (bf16[128,1024]{1,0:T(8,128)(2,1)S(1)}, bf16[128,1024]{1,0:T(8,128)(2,1)}, u32[]{:S(2)}) copy-start(bf16[128,1024]{1,0:T(8,128)(2,1)} %reduce-scatter.21.cloned.1.call-done) | copy-start | bytes 786436
  152.9 58.9 %copy-start.110 = (f32[128]{0:T(128)}, f32[128]{0:T(128)S(1)}, u32[]{:S(2)}) copy-start(f32[128]{0:T(128)S(1)} %get-tuple-element.168) | copy-start | bytes 1540
  155.2 35.9 %all-gather.20.cloned.1.call-start = ((), (), s32[]{:S(2)}) async-start(), calls=%async_computation.19 | async-start | bytes 1310720 | tf_op jit(solution)/shard_map/all_gather | solution.py:174
  156.0 76.5 %reduce-scatter.23.cloned.1.call-start = ((), (), s32[]{:S(2)}) async-start(), calls=%async_computation.20 | async-start | bytes 1310720 | tf_op jit(solution)/shard_map/reduce_scatter | solution.py:179
  156.0 123.3 %copy-start.93 = (f32[1024]{0:T(1024)}, f32[1024]{0:T(1024)S(1)}, u32[]{:S(2)}) copy-start(f32[1024]{0:T(1024)S(1)} %convert_element_type.389) | copy-start | bytes 12292
  207.5 52.3 %reduce-scatter.19.cloned.1.call-start = ((), (), s32[]{:S(2)}) async-start(), calls=%async_computation.17 | async-start | bytes 1310720 | tf_op jit(solution)/shard_map/reduce_scatter | solution.py:179
  211.7 67.6 %all-gather.16.cloned.1.call-start = ((), (), s32[]{:S(2)}) async-start(), calls=%async_computation.13 | async-start | bytes 1310720 | tf_op jit(solution)/shard_map/all_gather | solution.py:174
  262.4 53.7 %reduce-scatter.15.cloned.1.call-start = ((), (), s32[]{:S(2)}) async-start(), calls=%async_computation.14 | async-start | bytes 1310720 | tf_op jit(solution)/shard_map/reduce_scatter | solution.py:179
  291.0 49.2 %all-gather.22.cloned.1.call-start = ((), (), s32[]{:S(2)}) async-start(), calls=%async_computation.21 | async-start | bytes 1310720 | tf_op jit(solution)/shard_map/all_gather | solution.py:196
  323.4 35.1 %all-gather.30.cloned.1.call-start = ((), (), s32[]{:S(2)}) async-start(), calls=%async_computation.29 | async-start | bytes 1310720 | tf_op jit(solution)/shard_map/all_gather | solution.py:196
  327.1 49.5 %all-gather.26.cloned.1.call-start = ((), (), s32[]{:S(2)}) async-start(), calls=%async_computation.25 | async-start | bytes 1310720 | tf_op jit(solution)/shard_map/all_gather | solution.py:196
  329.7 87.5 %reduce-scatter.25.cloned.1.call-start = ((), (), s32[]{:S(2)}) async-start(), calls=%async_computation.22 | async-start | bytes 1310720 | tf_op jit(solution)/shard_map/reduce_scatter | solution.py:215
  392.1 52.5 %reduce-scatter.33.cloned.1.call-start = ((), (), s32[]{:S(2)}) async-start(), calls=%async_computation.30 | async-start | bytes 1310720 | tf_op jit(solution)/shard_map/reduce_scatter | solution.py:215
  395.7 76.3 %reduce-scatter.29.cloned.1.call-start = ((), (), s32[]{:S(2)}) async-start(), calls=%async_computation.26 | async-start | bytes 1310720 | tf_op jit(solution)/shard_map/reduce_scatter | solution.py:215
  399.3 91.6 %all-gather.24.cloned.1.call-start = ((), (), s32[]{:S(2)}) async-start(), calls=%async_computation.23 | async-start | bytes 1310720 | tf_op jit(solution)/shard_map/all_gather | solution.py:226
  422.0 96.2 %all-gather.28.cloned.1.call-start = ((), (), s32[]{:S(2)}) async-start(), calls=%async_computation.27 | async-start | bytes 1310720 | tf_op jit(solution)/shard_map/all_gather | solution.py:226
  479.3 63.3 %all-gather.32.cloned.1.call-start = ((), (), s32[]{:S(2)}) async-start(), calls=%async_computation.31 | async-start | bytes 1310720 | tf_op jit(solution)/shard_map/all_gather | solution.py:226
  487.5 171.4 %reduce-scatter.27.cloned.1.call-start = ((), (), s32[]{:S(2)}) async-start(), calls=%async_computation.24 | async-start | bytes 1310720 | tf_op jit(solution)/shard_map/reduce_scatter | solution.py:247
  518.1 142.2 %reduce-scatter.31.cloned.1.call-start = ((), (), s32[]{:S(2)}) async-start(), calls=%async_computation.28 | async-start | bytes 1310720 | tf_op jit(solution)/shard_map/reduce_scatter | solution.py:247
  551.9 109.8 %reduce-scatter.35.cloned.1.call-start = ((), (), s32[]{:S(2)}) async-start(), calls=%async_computation.32 | async-start | bytes 1310720 | tf_op jit(solution)/shard_map/reduce_scatter | solution.py:247
  578.8 253.5 %all-reduce.7.cloned.1.call-start = ((), (), s32[]{:S(2)}) async-start(), calls=%async_computation.36 | async-start | bytes 12582912 | tf_op jit(solution)/shard_map/psum | solution.py:300
  593.1 68.6 %copy-start.32 = (f32[128,1024]{1,0:T(8,128)S(1)}, f32[128,1024]{1,0:T(8,128)}, u32[]{:S(2)}) copy-start(f32[128,1024]{1,0:T(8,128)} %get-tuple-element.220) | copy-start | bytes 1572868
  593.1 68.6 %copy-start.108 = (f32[128]{0:T(128)S(1)}, f32[128]{0:T(128)}, u32[]{:S(2)}) copy-start(f32[128]{0:T(128)} %copy-done.107) | copy-start | bytes 1540
  662.8 173.0 %copy-start.75 = (bf16[1,3,128,1024]{3,2,1,0:T(8,128)(2,1)}, bf16[1,3,128,1024]{3,2,1,0:T(8,128)(2,1)S(1)}, u32[]{:S(2)}) copy-start(bf16[1,3,128,1024]{3,2,1,0:T(8,128)(2,1)S(1)} %fusion.101) | copy-start | bytes 2359300
  (114 other events, 631.3 us)
Sparse Core Ops, SparseCore 0:
  10.2 19.4 all-gather.37
  31.8 16.7 all-gather.33
  50.7 16.7 all-gather.35
  70.4 24.9 reduce-scatter.20
  98.5 24.8 reduce-scatter.12
  126.4 24.8 reduce-scatter.16
  155.3 16.7 all-gather.17
  174.3 16.7 all-gather.19
  207.6 24.8 reduce-scatter.22
  234.9 24.8 reduce-scatter.18
  262.5 16.7 all-gather.15
  291.1 24.8 reduce-scatter.14
  323.5 16.7 all-gather.21
  341.7 16.7 all-gather.29
  359.8 16.7 all-gather.25
  392.2 24.8 reduce-scatter.24
  419.7 24.8 reduce-scatter.32
  447.0 24.8 reduce-scatter.28
  474.2 16.7 all-gather.23
  492.4 16.7 all-gather.27
  510.8 16.7 all-gather.31
  530.8 24.9 reduce-scatter.26
  559.0 24.8 reduce-scatter.30
  586.4 25.0 reduce-scatter.34
  617.1 215.1 all-reduce.6

commit v2 on v0

v2 whole, which is shorter than its diff:
```python
import functools

import jax
import jax.numpy as jnp
from jax import lax
from jax.experimental import pallas as pl
from jax.experimental.pallas import tpu as pltpu
from jax.sharding import PartitionSpec as P

HD = 64
EPSILON = 1e-05
F32 = jnp.float32
LOW = jnp.bfloat16
MESH = pl.DeviceIdType.MESH
TILE = 256
PHASES = 4


def dot(left, right, left_dim=1, right_dim=0):
    return lax.dot_general(
        left, right, (((left_dim,), (right_dim,)), ((), ())), preferred_element_type=F32
    )


def row_sum(values):
    return jnp.sum(values, axis=0, keepdims=True)


def row_mean(values):
    return jnp.mean(values, axis=-1, keepdims=True)


def gelu_parts(h):
    t = 1.0 / (1.0 + 0.23164188 * jnp.abs(h))
    density = jnp.exp(-0.5 * h * h)
    series = t * (
        0.127414796
        + t * (-0.142248368 + t * (0.7107068705 + t * (-0.7265760135 + t * 0.5307027145)))
    )
    tail = series * density
    return jnp.where(h < 0.0, tail, 1.0 - tail), density * 0.3989422804014327


def layer_kernel(
    lengths_ref,
    x_ref,
    cot_ref,
    wqkv_ref,
    wout_ref,
    wup_ref,
    wdown_ref,
    vec_ref,
    out_ref,
    gin_ref,
    grads_ref,
    vgrad_ref,
    xa,
    wq,
    wo,
    wu,
    wd,
    qkv,
    pt,
    cc,
    ua,
    act,
    gp,
    g2a,
    g1a,
    dpr,
    part,
    rc,
    ys,
    ry,
    xh1,
    rstd1,
    resid,
    cot,
    gin,
    gb,
    vg,
    load_sem,
    store_sem,
    agy_send,
    agy_recv,
    agc_send,
    agc_recv,
    agf_send,
    agf_recv,
    rsc_send,
    rsc_recv,
    rsy_send,
    rsy_recv,
):
    batches = x_ref.shape[0]
    block = x_ref.shape[1]
    width = x_ref.shape[2]
    head_cols = wo.shape[0]
    hidden = wu.shape[1]
    rows = 4 * block
    pairs = head_cols // 128
    t = lax.axis_index("tensor")
    c = lax.rem(t, 2)
    y = lax.div(t, 2)
    t_core = y * 2 + (1 - c)
    t_y = (1 - y) * 2 + c
    t_far = (1 - y) * 2 + (1 - c)
    core = {"tensor": t_core}
    across = {"tensor": t_y}

    gathers = (xa, ua, g2a, g1a)

    def remote(src, dst, send, recv, device):
        return pltpu.make_async_remote_copy(
            src_ref=src, dst_ref=dst, send_sem=send, recv_sem=recv, device_id=device, device_id_type=MESH
        )

    def ag_y(p, s, at, src=None):
        buf = gathers[p]
        return remote(
            buf.at[s, at] if src is None else src, buf.at[s, at], agy_send.at[p, s], agy_recv.at[p, s], across
        )

    def ag_c(p, s, at, src=None):
        buf = gathers[p]
        return remote(
            buf.at[s, at] if src is None else src, buf.at[s, at], agc_send.at[p, s], agc_recv.at[p, s], core
        )

    def ag_f(p, s, at):
        buf = gathers[p]
        return remote(buf.at[s, at], buf.at[s, at], agf_send.at[p, s], agf_recv.at[p, s], core)

    def rs_c(p, s):
        return remote(part.at[s, 1 - c], rc.at[s], rsc_send.at[p, s], rsc_recv.at[p, s], core)

    def rs_y(p, s):
        return remote(ys.at[s], ry.at[s], rsy_send.at[p, s], rsy_recv.at[p, s], across)

    def load(index, src, dst):
        return pltpu.make_async_copy(src, dst, load_sem.at[index])

    def store(index, src, dst):
        return pltpu.make_async_copy(src, dst, store_sem.at[index])

    loads = [load(s, x_ref.at[s], xa.at[s, t]) for s in range(batches)]
    n = batches
    load_wq = load(n, wqkv_ref, wq)
    load_wo = load(n + 1, wout_ref, wo)
    load_wu = load(n + 2, wup_ref, wu)
    load_wd = load(n + 3, wdown_ref, wd)
    load_cot = load(n + 4, cot_ref, cot)

    barrier = pltpu.get_barrier_semaphore()
    for device in (core, across):
        pl.semaphore_signal(barrier, inc=1, device_id=device, device_id_type=MESH)
    for cp in loads:
        cp.start()
    load_wq.start()
    load_wo.start()
    pl.semaphore_wait(barrier, 2)
    for s in range(batches):
        ag_y(0, s, t, x_ref.at[s]).start()
        ag_c(0, s, t, x_ref.at[s]).start()
    load_wu.start()
    load_wd.start()
    load_cot.start()

    vg[...] = jnp.zeros_like(vg)
    lane = lax.broadcasted_iota(jnp.int32, (rows, 128), 1)
    low_half = lane < HD
    empty = jnp.zeros((rows, 128), LOW)

    def masked(values, h):
        return jnp.where(low_half, values, empty) if h == 0 else jnp.where(low_half, empty, values)

    def vec(i):
        return vec_ref[i : i + 1, :]

    def whole(ref, s):
        return ref[s].reshape(rows, width)

    def put_part(s, j, values):
        values = values.astype(LOW)
        for b in range(4):
            part[s, b % 2, b // 2, :, j * TILE : (j + 1) * TILE] = values[b * block : (b + 1) * block]

    def compute_a(s):
        tokens = whole(xa, s)
        q = dot(tokens, wq[0]) + vec_ref[7:8, :head_cols]
        qkv[s, 0] = q.astype(LOW) * LOW(HD ** (-0.5))
        qkv[s, 1] = dot(tokens, wq[1]).astype(LOW)
        v = dot(tokens, wq[2]) + vec_ref[7:8, head_cols : 2 * head_cols]
        qkv[s, 2] = v.astype(LOW)
        keys_valid = lax.broadcasted_iota(jnp.int32, (rows, rows), 0) < lengths_ref[0, s]
        for j in range(pairs):
            cols = slice(j * 128, (j + 1) * 128)
            q, k, v = qkv[s, 0, :, cols], qkv[s, 1, :, cols], qkv[s, 2, :, cols]
            context = jnp.zeros((128, rows), F32)
            for h in range(2):
                scores = dot(k, masked(q, h), 1, 1)
                scores = jnp.where(keys_valid, scores, -1e30)
                weights = jnp.exp(scores - jnp.max(scores, axis=0, keepdims=True))
                p = (weights * (1.0 / row_sum(weights))).astype(LOW)
                pt[s, 2 * j + h] = p
                context = context + dot(masked(v, h).T, p)
            cc[s, :, cols] = context.T.astype(LOW)
        context = cc[s]
        for j in range(width // TILE):
            put_part(s, j, dot(context, wo[:, j * TILE : (j + 1) * TILE]))

    def compute_c(s):
        normed = whole(ua, s)
        for j in range(hidden // TILE):
            cols = slice(j * TILE, (j + 1) * TILE)
            h = dot(normed, wu[:, cols]) + vec_ref[6:7, cols]
            phi, density = gelu_parts(h)
            act[s, :, cols] = (h * phi).astype(LOW)
            gp[s, :, cols] = (phi + h * density).astype(LOW)
        activated = act[s]
        for j in range(width // TILE):
            put_part(s, j, dot(activated, wd[:, j * TILE : (j + 1) * TILE]))

    def compute_e(s):
        grad = whole(g2a, s)
        for j in range(hidden // TILE):
            cols = slice(j * TILE, (j + 1) * TILE)
            gh = gp[s, :, cols].astype(F32) * dot(grad, wd[cols, :], 1, 1)
            vg[6:7, cols] += row_sum(gh)
            gp[s, :, cols] = gh.astype(LOW)
        grad_hidden = gp[s]
        for j in range(width // TILE):
            put_part(s, j, dot(grad_hidden, wu[j * TILE : (j + 1) * TILE, :], 1, 1))

    def compute_g(s):
        grad_context = dot(whole(g1a, s), wo[...], 1, 1).astype(LOW)
        for j in range(pairs):
            cols = slice(j * 128, (j + 1) * 128)
            q, k, v = qkv[s, 0, :, cols], qkv[s, 1, :, cols], qkv[s, 2, :, cols]
            gc = grad_context[:, cols]
            dq = jnp.zeros((128, rows), F32)
            dk = jnp.zeros((rows, 128), F32)
            dv = jnp.zeros((rows, 128), F32)
            for h in range(2):
                gc_h = masked(gc, h)
                p = pt[s, 2 * j + h]
                wide = p.astype(F32)
                product = wide * dot(v, gc_h, 1, 1)
                ds = (product - wide * row_sum(product)).astype(LOW)
                dv = dv + dot(p, gc_h)
                dk = dk + dot(ds, masked(q, h))
                dq = dq + dot(masked(k, h).T, ds)
            dq = dq.T * (HD ** (-0.5))
            vg[7:8, cols] += row_sum(dq)
            vg[7:8, head_cols + j * 128 : head_cols + (j + 1) * 128] += row_sum(dv)
            dpr[s, 0, :, cols] = dq.astype(LOW)
            dpr[s, 1, :, cols] = dk.astype(LOW)
            dpr[s, 2, :, cols] = dv.astype(LOW)
        for j in range(width // TILE):
            at = slice(j * TILE, (j + 1) * TILE)
            total = dot(dpr[s, 0], wq[0, at, :], 1, 1)
            total = total + dot(dpr[s, 1], wq[1, at, :], 1, 1)
            total = total + dot(dpr[s, 2], wq[2, at, :], 1, 1)
            put_part(s, j, total)

    computes = (compute_a, compute_c, compute_e, compute_g)

    def reduced(p, s):
        rs_y(p, s).wait()
        rs_c(p, s).wait_send()
        return part[s, c, y].astype(F32) + rc[s, y].astype(F32) + ry[s].astype(F32)

    def send_on(p, s):
        ag_y(p, s, t).start()
        ag_c(p, s, t).start()

    def finish_a(s):
        z = xa[s, t].astype(F32) + (reduced(0, s) + vec(0))
        centred = z - row_mean(z)
        rstd = lax.rsqrt(row_mean(centred * centred) + EPSILON)
        hat = centred * rstd
        xh1[s] = hat
        rstd1[s] = jnp.broadcast_to(rstd, rstd1.shape[1:])
        ua[s, t] = (hat * vec(1) + vec(2)).astype(LOW)
        send_on(1, s)

    def finish_c(s):
        z = (xh1[s] * vec(1) + vec(2)) + (reduced(1, s) + vec(3))
        centred = z - row_mean(z)
        rstd = lax.rsqrt(row_mean(centred * centred) + EPSILON)
        hat = centred * rstd
        valid = t * block + lax.broadcasted_iota(jnp.int32, (block, width), 0) < lengths_ref[0, s]
        incoming = jnp.where(valid, cot[s].astype(F32), 0.0)
        scaled = incoming * vec(4)
        grad = rstd * (scaled - row_mean(scaled) - hat * row_mean(scaled * hat))
        resid[s] = grad
        g2a[s, t] = grad.astype(LOW)
        send_on(2, s)
        cot[s] = jnp.where(valid, hat * vec(4) + vec(5), 0.0).astype(LOW)
        store(s, cot.at[s], out_ref.at[s]).start()
        vg[3:4, :] += row_sum(grad)
        vg[4:5, :] += row_sum(incoming * hat)
        vg[5:6, :] += row_sum(incoming)

    def finish_e(s):
        gu = resid[s] + reduced(2, s)
        hat = xh1[s]
        scaled = gu * vec(1)
        grad = rstd1[s, :, :1] * (scaled - row_mean(scaled) - hat * row_mean(scaled * hat))
        resid[s] = grad
        g1a[s, t] = grad.astype(LOW)
        send_on(3, s)
        vg[0:1, :] += row_sum(grad)
        vg[1:2, :] += row_sum(gu * hat)
        vg[2:3, :] += row_sum(gu)

    def finish_g(s):
        gin[s] = (resid[s] + reduced(3, s)).astype(LOW)
        store(batches + s, gin.at[s], gin_ref.at[s]).start()

    finishes = (finish_a, finish_c, finish_e, finish_g)

    def forward_block(p, s):
        ag_y(p, s, t_y).wait_recv()
        ag_f(p, s, t_y).start()

    def slot(p, s):
        ag_c(p, s, t_core).wait_recv()
        ag_f(p, s, t_far).wait_recv()
        computes[p](s)
        rs_c(p, s).start()
        rs_c(p, s).wait_recv()
        ys[s] = (part[s, c, 1 - y].astype(F32) + rc[s, 1 - y].astype(F32)).astype(LOW)
        rs_y(p, s).start()

    forward_block(0, 0)
    for p in range(PHASES):
        if p == 0:
            for cp in loads:
                cp.wait()
            load_wq.wait()
            load_wo.wait()
        if p == 1:
            load_wu.wait()
            load_wd.wait()
            load_cot.wait()

        def step(s, carry, p=p):
            slot(p, s)
            if p > 0:

                @pl.when(s == 0)
                def _():
                    finishes[p - 1](batches - 1)

            @pl.when(s > 0)
            def _():
                finishes[p](s - 1)

            @pl.when(s < batches - 1)
            def _():
                forward_block(p, s + 1)

            if p < PHASES - 1:

                @pl.when(s == batches - 1)
                def _():
                    forward_block(p + 1, 0)

            return carry

        lax.fori_loop(0, batches, step, 0)
    def tall(ref):
        return ref[...].reshape(batches * rows, -1)

    chunk = 0
    grads2 = tall(g2a)
    for j in range(hidden // TILE):
        a = act[:, :, j * TILE : (j + 1) * TILE].reshape(batches * rows, TILE)
        gb[chunk] = dot(a, grads2, 0, 0).astype(LOW)
        store(2 * batches + chunk, gb.at[chunk], grads_ref.at[chunk]).start()
        chunk += 1
    gradh = tall(gp)
    for j in range(width // TILE):
        a = ua[:, :, :, j * TILE : (j + 1) * TILE].reshape(batches * rows, TILE)
        gb[chunk] = dot(a, gradh, 0, 0).astype(LOW)
        store(2 * batches + chunk, gb.at[chunk], grads_ref.at[chunk]).start()
        chunk += 1
    gb[chunk] = dot(tall(cc), tall(g1a), 0, 0).astype(LOW)
    store(2 * batches + chunk, gb.at[chunk], grads_ref.at[chunk]).start()
    chunk += 1
    for i in range(3):
        d = dpr[:, i].reshape(batches * rows, head_cols)
        for j in range(width // TILE):
            a = xa[:, :, :, j * TILE : (j + 1) * TILE].reshape(batches * rows, TILE)
            gb[chunk, :, j * TILE : (j + 1) * TILE] = dot(a, d, 0, 0).astype(LOW)
        store(2 * batches + chunk, gb.at[chunk], grads_ref.at[chunk]).start()
        chunk += 1
    finishes[PHASES - 1](batches - 1)
    vgrad_ref[...] = vg[...]
    for s in range(batches):
        store(s, cot.at[s], out_ref.at[s]).wait()
        store(batches + s, gin.at[s], gin_ref.at[s]).wait()
    for i in range(chunk):
        store(2 * batches + i, gb.at[i], grads_ref.at[i]).wait()

    def drain(i, carry):
        for p in range(PHASES):
            ag_y(p, i, t).wait_send()
            ag_c(p, i, t).wait_send()
            ag_f(p, i, t_y).wait_send()
        return carry

    lax.fori_loop(0, batches, drain, 0)


def run_layer(lengths, x, cot, wqkv, wout, wup, wdown, vec):
    batches, block, width = x.shape
    rows = 4 * block
    head_cols = wout.shape[0]
    heads = head_cols // HD
    hidden = wup.shape[1]
    chunks = hidden // TILE + width // TILE + 1 + 3
    any_space = pl.BlockSpec(memory_space=pl.ANY)
    vmem = pl.BlockSpec(memory_space=pltpu.VMEM)
    dma = pltpu.SemaphoreType.DMA
    low = lambda *shape: pltpu.VMEM(shape, LOW)
    wide = lambda *shape: pltpu.VMEM(shape, F32)
    gathered = low(batches, 4, block, width)
    scratch = [
        gathered,
        low(3, width, head_cols),
        low(head_cols, width),
        low(width, hidden),
        low(hidden, width),
        low(batches, 3, rows, head_cols),
        low(batches, heads, rows, rows),
        low(batches, rows, head_cols),
        gathered,
        low(batches, rows, hidden),
        low(batches, rows, hidden),
        gathered,
        gathered,
        low(batches, 3, rows, head_cols),
        low(batches, 2, 2, block, width),
        low(batches, 2, block, width),
        low(batches, block, width),
        low(batches, block, width),
        wide(batches, block, width),
        wide(batches, block, 128),
        wide(batches, block, width),
        low(batches, block, width),
        low(batches, block, width),
        low(chunks, TILE, width),
        wide(8, width),
        dma((batches + 5,)),
        dma((2 * batches + chunks,)),
    ] + [dma((PHASES, batches))] * 10
    return pl.pallas_call(
        layer_kernel,
        out_shape=(
            jax.ShapeDtypeStruct((batches, block, width), LOW),
            jax.ShapeDtypeStruct((batches, block, width), LOW),
            jax.ShapeDtypeStruct((chunks, TILE, width), LOW),
            jax.ShapeDtypeStruct((8, width), F32),
        ),
        in_specs=[pl.BlockSpec(memory_space=pltpu.SMEM)] + [any_space] * 6 + [vmem],
        out_specs=(any_space, any_space, any_space, vmem),
        scratch_shapes=scratch,
        compiler_params=pltpu.CompilerParams(
            collective_id=0, has_side_effects=True, vmem_limit_bytes=62 << 20
        ),
        name="layer",
    )(lengths, x, cot, wqkv, wout, wup, wdown, vec)


def per_device(
    inputs,
    lengths,
    cotangent,
    w_qkv,
    b_query,
    b_value,
    w_out,
    b_out,
    ln1_gain,
    ln1_bias,
    w_up,
    b_up,
    w_down,
    b_down,
    ln2_gain,
    ln2_bias,
):
    width = inputs.shape[3]
    head_cols = w_out.shape[0]
    hidden = w_up.shape[1]
    narrow = jnp.concatenate([b_query, b_value, jnp.zeros((width - 2 * head_cols,), LOW)])
    vec = jnp.stack([b_out, ln1_gain, ln1_bias, b_down, ln2_gain, ln2_bias, b_up, narrow]).astype(F32)
    output, grad_inputs, grads, vgrad = run_layer(
        lengths,
        inputs[0],
        cotangent[0],
        jnp.transpose(w_qkv, (1, 0, 2)),
        w_out,
        w_up,
        w_down,
        vec,
    )
    grads = lax.psum(grads, "dp").astype(F32)
    shared = lax.psum(vgrad[:6], ("dp", "tensor"))
    split = lax.psum(vgrad[6:], "dp")
    down = hidden // TILE
    up = down + width // TILE
    grad_down = grads[:down].reshape(hidden, width)
    grad_up = grads[down:up].reshape(width, hidden)
    grad_out = grads[up]
    grad_qkv = grads[up + 1 :].reshape(3, TILE, width // TILE, head_cols)
    grad_qkv = jnp.transpose(grad_qkv, (2, 1, 0, 3)).reshape(width, 3, head_cols)
    return (
        output[None],
        grad_inputs[None],
        grad_qkv,
        split[1, :head_cols],
        split[1, head_cols : 2 * head_cols],
        grad_out,
        shared[0],
        shared[1],
        shared[2],
        grad_up,
        split[0],
        grad_down,
        shared[3],
        shared[4],
        shared[5],
    )


def solution(mesh):
    return jax.shard_map(
        per_device,
        mesh=mesh,
        in_specs=(
            P("dp", None, "tensor", None),
            P("dp", None),
            P("dp", None, "tensor", None),
            P(None, None, "tensor"),
            P("tensor"),
            P("tensor"),
            P("tensor", None),
            P(),
            P(),
            P(),
            P(None, "tensor"),
            P("tensor"),
            P("tensor", None),
            P(),
            P(),
            P(),
        ),
        out_specs=(
            P("dp", None, "tensor", None),
            P("dp", None, "tensor", None),
            P(None, None, "tensor"),
            P("tensor"),
            P("tensor"),
            P("tensor", None),
            P(),
            P(),
            P(),
            P(None, "tensor"),
            P("tensor"),
            P("tensor", None),
            P(),
            P(),
            P(),
        ),
        check_vma=False,
    )
```

time: 1150 us -> 405 us (0.35)
  waiting for transfers between devices: 778 us -> 150 us
  matrix products: 156 us -> 0 us
  Pallas kernels: 0 us -> 149 us
  other arithmetic: 62.9 us -> 2.85 us
  local copies, waits for them, and re-layouts: 45.9 us -> 25.4 us
  loops' own time: 16.8 us -> 0 us
    reduce_scatter x12 -> x0, waiting for transfers between devices: 251 us -> none  [the longest x3 75 us: micro_batch(): lax.psum_scatter(jnp.einsum('sf,df->sd', grad_hidden_low, w_up, preferred...]
    psum x1, waiting for transfers between devices: 342 us -> 150 us  [per_device(): grads = lax.psum(grads, 'dp').astype(F32)]
    all_gather x12 -> x0, waiting for transfers between devices: 184 us -> none  [the longest x3 50.4 us: micro_batch(): lax.all_gather(normed.astype(jnp.bfloat16), 'tensor', axis=0, tiled=True)]
    dot_general x54 -> x0, matrix products: 156 us -> none  [the longest x3 26 us: micro_batch(): jnp.dot(normed_all, w_up, preferred_element_type=jnp.float32) + b_up]
    pallas_call x0 -> x1, Pallas kernels: none -> 149 us  [run_layer(): pl.pallas_call(layer_kernel, out_shape=(jax.ShapeDtypeStruct((batches, bl...]
    reduce_sum x30 -> x0, other arithmetic: 34 us -> none  [the longest x6 9.31 us: layer_norm(): return centred * lax.rsqrt(spread + EPSILON) * norm_gain + norm_shift]
    unnamed x134 -> x10, local copies, waits for them, and re-layouts: 21.3 us -> 4.2 us
    another operation x1 -> x0, loops' own time: 16.8 us -> none  [per_device(): lax.fori_loop(0, batches - 1, lambda batch_index, state_now: micro_batch(...]
  transfers between devices with their start and end apart: 25 -> 1, of which waited for: 24 -> 1; matrix products, arithmetic and copies ran while one was open for 6% -> 0% of each run, Pallas kernels for 0% -> 0%
where the time goes in v2:
time: 405 us; the launch traced here: 404 us
  waiting for transfers between devices  150 us (37%)
  Pallas kernels  149 us (37%)
  blocking collectives  62.7 us (15%)
  local copies, waits for them, and re-layouts  25.4 us (6%)
  between operations  14.1 us (3%)
    psum x1, waiting for transfers between devices, per_device(): grads = lax.psum(grads, 'dp').astype(F32)  150 us
    pallas_call x1, Pallas kernels, run_layer(): pl.pallas_call(layer_kernel, out_shape=(jax.ShapeDtypeStruct((batches, bl...  149 us
    psum x1, blocking collectives, per_device(): shared = lax.psum(vgrad[:6], ('dp', 'tensor'))  39.7 us
    psum x1, blocking collectives, per_device(): split = lax.psum(vgrad[6:], 'dp')  23.1 us
  transfers between devices with their start and end apart: 1, of which 1 were waited for; matrix products, arithmetic and copies ran while one was open for 0% of the time, Pallas kernels for 0%

profile of v2, /device:TPU:0, one launch (start us, length us, event | category | flops | bytes accessed | tf_op | source)
XLA Modules:
  0.0 404.4 jit_solution(14390851681521669528)
XLA Ops:
  7.2 0.0 all-reduce.2.cloned.1.call-start
  7.2 0.7 stack.27
  7.9 0.7 stack.28
  8.6 0.7 stack.29
  9.3 0.7 stack.30
  10.0 0.7 stack.31
  10.7 0.7 stack.32
  11.3 0.7 stack.33
  12.0 0.7 pad_maximum_fusion
  12.7 0.1 stack.35
  12.8 0.6 convert_element_type.6.vec_ref
  13.4 149.2 %layer.1 = (bf16[3,128,1024]{2,1,0:T(8,128)(2,1)}, bf16[3,128,1024]{2,1,0:T(8,128)(2,1)}, bf16[12,256,1024]{2,1,0:T(8,128)(2,1)}, f32[8,1024]{1,0:T(8,128)}) custom-call(s32[1,3]{1,0:T(1,128)} %lengths_ref.1, bf16[3,128,1024]{2,1,0:T(8,128)(2,1)} %bitcast.28, bf16[3,128,1024]{2,1,0:T(8,128)(2,1)} %bitcast.29, bf16[3,1024,256]{2,1,0:T(8,128)(2,1)} %bitcast.25, ...), custom_call_target="tpu_custom_call" | custom-call | tf_op jit(solution)/shard_map/layer/pallas_call | solution.py:459
  162.6 0.0 copy-start.3
  162.6 0.0 all-reduce.2.cloned.1.call-update
  162.6 0.7 copy-done.3
  163.4 23.1 %psum.22 = f32[2,1024]{1,0:T(2,128)S(1)} all-reduce(f32[2,1024]{1,0:T(2,128)S(1)} %slice.46), channel_id=1, replica_groups=mesh['dp'=8,'tensor'=4] {'dp'}, use_global_device_ids=true, to_apply=%region_1.0 | all-reduce | flops 2048 | bytes 16384 | tf_op jit(solution)/shard_map/psum | solution.py:512
  186.4 0.6 slice.68
  187.0 39.7 %psum.23 = f32[6,1024]{1,0:T(8,128)S(1)} all-reduce(f32[6,1024]{1,0:T(8,128)S(1)} %bitcast.30), channel_id=1, replica_groups=mesh['dp'=8,'tensor'=4] {'dp','tensor'}, use_global_device_ids=true, to_apply=%region_2.0 | all-reduce | flops 6144 | bytes 49152 | tf_op jit(solution)/shard_map/psum | solution.py:511
  226.7 0.6 fusion.2
  227.3 0.6 fusion.1
  227.9 150.0 %all-reduce.2.cloned.1.call-done = bf16[12,256,1024]{2,1,0:T(8,128)(2,1)} async-done(((bf16[12,256,1024]{2,1,0:T(8,128)(2,1)}), bf16[12,256,1024]{2,1,0:T(8,128)(2,1)}) %all-reduce.2.cloned.1.call-update) | async-done | bytes 6291472 | tf_op jit(solution)/shard_map/psum | solution.py:510
  377.9 3.5 slice.60
  381.4 3.4 reshape.42
  384.8 0.0 copy-start
  384.8 2.2 copy.31
  387.0 1.7 copy-done
  388.7 1.6 convert_element_type.7
  390.3 1.0 slice_bitcast_fusion
  391.3 4.4 %fusion = (f32[4,256,1024]{2,1,0:T(8,128)}, f32[4,256,1024]{2,1,0:T(8,128)}) fusion(bf16[12,256,1024]{2,1,0:T(8,128)(2,1)S(1)} %copy-done), kind=kLoop, calls=%fused_computation.2 | loop fusion | bytes 16777216 | tf_op jit(solution)/shard_map/slice | solution.py:515
  395.8 0.9 copy.35
  396.7 0.0 copy-done.1
  396.7 0.9 copy.36
  (6 shorter events, 0.0 us)
Async XLA Ops:
  7.2 370.7 %all-reduce.2.cloned.1.call-start = ((), (), s32[]{:S(2)}) async-start(), calls=%async_computation | async-start | bytes 12582912 | tf_op jit(solution)/shard_map/psum | solution.py:510
  162.6 0.8 copy-start.3
  384.8 3.9 copy-start
  391.3 4.4 %copy-start.2 = (bf16[3,128,1024]{2,1,0:T(8,128)(2,1)S(1)}, bf16[3,128,1024]{2,1,0:T(8,128)(2,1)}, u32[]{:S(2)}) copy-start(bf16[3,128,1024]{2,1,0:T(8,128)(2,1)} %get-tuple-element.19) | copy-start | bytes 2359300
  391.3 5.3 %copy-start.1 = (bf16[3,128,1024]{2,1,0:T(8,128)(2,1)S(1)}, bf16[3,128,1024]{2,1,0:T(8,128)(2,1)}, u32[]{:S(2)}) copy-start(bf16[3,128,1024]{2,1,0:T(8,128)(2,1)} %get-tuple-element.20) | copy-start | bytes 2359300
Sparse Core Ops, SparseCore 0:
  162.7 215.1 all-reduce.1

commit v3 on v2

--- a/solution.py
+++ b/solution.py
@@ -13,6 +13,7 @@
 LOW = jnp.bfloat16
 MESH = pl.DeviceIdType.MESH
 TILE = 256
+UNIT = 64
 PHASES = 4
 
 
@@ -389,11 +390,16 @@
     gb[chunk] = dot(tall(cc), tall(g1a), 0, 0).astype(LOW)
     store(2 * batches + chunk, gb.at[chunk], grads_ref.at[chunk]).start()
     chunk += 1
+    fold = width // head_cols
     for i in range(3):
         d = dpr[:, i].reshape(batches * rows, head_cols)
         for j in range(width // TILE):
             a = xa[:, :, :, j * TILE : (j + 1) * TILE].reshape(batches * rows, TILE)
-            gb[chunk, :, j * TILE : (j + 1) * TILE] = dot(a, d, 0, 0).astype(LOW)
+            product = dot(a, d, 0, 0).astype(LOW)
+            for h in range(TILE // UNIT):
+                piece = j * (TILE // UNIT) + h
+                at, col = piece // fold * UNIT, piece % fold * head_cols
+                gb[chunk, at : at + UNIT, col : col + head_cols] = product[h * UNIT : (h + 1) * UNIT]
         store(2 * batches + chunk, gb.at[chunk], grads_ref.at[chunk]).start()
         chunk += 1
     finishes[PHASES - 1](batches - 1)
@@ -474,6 +480,384 @@
     )(lengths, x, cot, wqkv, wout, wup, wdown, vec)
 
 
+HOPS = 11
+
+
+class Reducer:
+    def __init__(self, gb, rx, rz, rm, rb, rn, rq, send_sems, recv_sems):
+        dp = lax.axis_index("dp")
+        self.x = lax.rem(dp, 2)
+        self.z = lax.div(dp, 2)
+        self.side = lax.rem(self.z, 2)
+        self.m = lax.div(self.z, 2)
+        self.inner = self.side != self.m
+        self.outer = self.side == self.m
+        self.to_x = {"dp": self.z * 2 + (1 - self.x)}
+        self.to_pair = {"dp": (self.z + 1 - 2 * self.side) * 2 + self.x}
+        self.to_mid = {"dp": (3 - self.z) * 2 + self.x}
+        self.gb, self.rx, self.rz, self.rm, self.rb, self.rn, self.rq = gb, rx, rz, rm, rb, rn, rq
+        self.send_sems, self.recv_sems = send_sems, recv_sems
+
+    def greet(self, extra=()):
+        barrier = pltpu.get_barrier_semaphore()
+
+        def signal(device):
+            pl.semaphore_signal(barrier, inc=1, device_id=device, device_id_type=MESH)
+
+        for device in (self.to_x, self.to_pair) + tuple(extra):
+            signal(device)
+
+        @pl.when(self.inner)
+        def _():
+            signal(self.to_mid)
+            pl.semaphore_wait(barrier, 3 + len(extra))
+
+        @pl.when(self.outer)
+        def _():
+            pl.semaphore_wait(barrier, 2 + len(extra))
+
+    def copy(self, hop, k, src, dst, device):
+        return pltpu.make_async_remote_copy(
+            src_ref=src,
+            dst_ref=dst,
+            send_sem=self.send_sems.at[hop, k],
+            recv_sem=self.recv_sems.at[hop, k],
+            device_id=device,
+            device_id_type=MESH,
+        )
+
+    def ax(self, k):
+        return self.copy(0, k, self.gb.at[2 * k, 1 - self.x], self.rx.at[k, 1 - self.x], self.to_x)
+
+    def az(self, k):
+        return self.copy(1, k, self.gb.at[2 * k, self.x], self.rz.at[k], self.to_pair)
+
+    def am(self, k):
+        return self.copy(2, k, self.gb.at[2 * k, self.x], self.rm.at[k], self.to_mid)
+
+    def ao(self, k):
+        return self.copy(3, k, self.rx.at[k, self.x], self.rx.at[k, self.x], self.to_pair)
+
+    def ag(self, k):
+        return self.copy(4, k, self.rx.at[k, self.x], self.rx.at[k, self.x], self.to_x)
+
+    def bi(self, k):
+        return self.copy(5, k, self.gb.at[2 * k + 1], self.rb.at[k], self.to_pair)
+
+    def bm(self, k):
+        return self.copy(6, k, self.gb.at[2 * k + 1, 1 - self.m], self.rn.at[k], self.to_mid)
+
+    def bx(self, k):
+        return self.copy(7, k, self.gb.at[2 * k + 1, self.m], self.rq.at[k], self.to_x)
+
+    def bg(self, k):
+        return self.copy(8, k, self.rb.at[k, self.m], self.rb.at[k, self.m], self.to_mid)
+
+    def bo(self, k):
+        return self.copy(9, k, self.rb.at[k, self.m], self.rb.at[k, self.m], self.to_pair)
+
+    def bp(self, k):
+        return self.copy(10, k, self.rb.at[k, 1 - self.m], self.rb.at[k, 1 - self.m], self.to_pair)
+
+    def add(self, out, left, right):
+        out[...] = (left[...].astype(F32) + right[...].astype(F32)).astype(LOW)
+
+    def start(self, k):
+        self.ax(k).start()
+
+        @pl.when(self.outer)
+        def _():
+            self.bi(k).start()
+
+    def stage1(self, k):
+        self.ax(k).wait()
+        own = self.gb.at[2 * k, self.x]
+        self.add(own, own, self.rx.at[k, self.x])
+
+        @pl.when(self.outer)
+        def _():
+            self.az(k).start()
+
+    def stage2(self, k):
+        @pl.when(self.inner)
+        def _():
+            self.bi(k).wait_recv()
+            away = self.gb.at[2 * k + 1, 1 - self.m]
+            self.add(away, away, self.rb.at[k, 1 - self.m])
+            self.bm(k).start()
+            own = self.gb.at[2 * k + 1, self.m]
+            self.add(own, own, self.rb.at[k, self.m])
+            self.az(k).wait_recv()
+            own = self.gb.at[2 * k, self.x]
+            self.add(own, own, self.rz.at[k])
+            self.am(k).start()
+
+    def stage3(self, k):
+        @pl.when(self.inner)
+        def _():
+            self.bm(k).wait()
+            own = self.gb.at[2 * k + 1, self.m]
+            self.add(own, own, self.rn.at[k])
+            self.bx(k).start()
+            self.am(k).wait()
+            self.add(self.rx.at[k, self.x], self.gb.at[2 * k, self.x], self.rm.at[k])
+            self.ao(k).start()
+            self.ag(k).start()
+
+    def stage4(self, k):
+        @pl.when(self.inner)
+        def _():
+            self.bx(k).wait()
+            self.add(self.rb.at[k, self.m], self.gb.at[2 * k + 1, self.m], self.rq.at[k])
+            self.bg(k).start()
+            self.bo(k).start()
+
+        @pl.when(self.outer)
+        def _():
+            self.ao(k).wait_recv()
+            self.ag(k).start()
+
+    def stage5(self, k):
+        @pl.when(self.inner)
+        def _():
+            self.bg(k).wait_recv()
+            self.bp(k).start()
+
+        self.ag(k).wait_recv()
+
+    def stage6(self, k):
+        @pl.when(self.outer)
+        def _():
+            self.bo(k).wait_recv()
+            self.bp(k).wait_recv()
+
+    def drain(self, k):
+        self.ag(k).wait_send()
+
+        @pl.when(self.inner)
+        def _():
+            self.ao(k).wait_send()
+            self.bg(k).wait_send()
+            self.bo(k).wait_send()
+            self.bp(k).wait_send()
+
+        @pl.when(self.outer)
+        def _():
+            self.az(k).wait_send()
+            self.bi(k).wait_send()
+
+    stages = (stage1, stage2, stage3, stage4, stage5, stage6)
+
+
+VECTOR_HOPS = 6
+
+
+class VectorReducer:
+    def __init__(self, reducer, held, landed, send_sem, recv_sem, shared):
+        t = lax.axis_index("tensor")
+        c = lax.rem(t, 2)
+        y = lax.div(t, 2)
+        self.r = reducer
+        self.held, self.landed, self.send_sem, self.recv_sem = held, landed, send_sem, recv_sem
+        self.shared = shared
+        self.devices = (
+            {"tensor": y * 2 + (1 - c)},
+            {"tensor": (1 - y) * 2 + c},
+            reducer.to_x,
+            reducer.to_pair,
+            reducer.to_mid,
+            reducer.to_pair,
+        )
+
+    def copy(self, hop):
+        src = self.held.at[5 if hop == 5 else hop]
+        dst = self.held.at[5] if hop == 5 else self.landed.at[hop]
+        return pltpu.make_async_remote_copy(
+            src_ref=src,
+            dst_ref=dst,
+            send_sem=self.send_sem.at[hop],
+            recv_sem=self.recv_sem.at[hop],
+            device_id=self.devices[hop],
+            device_id_type=MESH,
+        )
+
+    def begin(self, hop):
+        if hop < 3:
+            self.copy(hop).start()
+        else:
+
+            @pl.when(self.r.outer if hop == 3 else self.r.inner)
+            def _():
+                self.copy(hop).start()
+
+    def end(self, hop):
+        if hop < 3:
+            self.copy(hop).wait()
+            got = self.landed[hop]
+            if hop < 2:
+                row = lax.broadcasted_iota(jnp.int32, got.shape, 0)
+                got = jnp.where(row < self.shared, got, 0.0)
+            self.held[hop + 1] = self.held[hop] + got
+        elif hop == 3:
+
+            @pl.when(self.r.outer)
+            def _():
+                self.copy(3).wait_send()
+
+            @pl.when(self.r.inner)
+            def _():
+                self.copy(3).wait_recv()
+                self.held[4] = self.held[3] + self.landed[3]
+
+        elif hop == 4:
+
+            @pl.when(self.r.inner)
+            def _():
+                self.copy(4).wait()
+                self.held[5] = self.held[4] + self.landed[4]
+
+        else:
+
+            @pl.when(self.r.inner)
+            def _():
+                self.copy(5).wait_send()
+
+            @pl.when(self.r.outer)
+            def _():
+                self.copy(5).wait_recv()
+
+
+def sum_kernel(
+    grads_ref, vgrad_ref, gdown_ref, gup_ref, gout_ref, gqkv_ref, vsum_ref,
+    gb, rx, rz, rm, rb, rn, rq, held, landed, load_sem, store_sem, send_sems, recv_sems, vsend, vrecv,
+):
+    chunks = gb.shape[0]
+    pairs = chunks // 2
+    rows = 2 * gb.shape[2]
+    reducer = Reducer(gb, rx, rz, rm, rb, rn, rq, send_sems, recv_sems)
+    vectors = VectorReducer(reducer, held, landed, vsend, vrecv, 6)
+
+    def load(k):
+        return pltpu.make_async_copy(grads_ref.at[pl.ds(2 * k, 2)], gb.at[pl.ds(2 * k, 2)], load_sem.at[k])
+
+    for k in range(pairs):
+        load(k).start()
+    held[0] = vgrad_ref[...]
+    reducer.greet(vectors.devices[:2])
+    n = len(reducer.stages)
+    ahead = 2
+    for k in range(ahead):
+        load(k).wait()
+        reducer.start(k)
+    vectors.begin(0)
+
+    def tick(now, carry):
+        @pl.when(now + ahead < pairs)
+        def _():
+            load(now + ahead).wait()
+            reducer.start(now + ahead)
+
+        for i in range(n):
+            k = now - i
+
+            @pl.when(jnp.logical_and(k >= 0, k < pairs))
+            def _():
+                reducer.stages[i](reducer, k)
+
+        for hop in range(VECTOR_HOPS):
+
+            @pl.when(now == hop)
+            def _():
+                vectors.end(hop)
+                if hop + 1 < VECTOR_HOPS:
+                    vectors.begin(hop + 1)
+
+        return carry
+
+    lax.fori_loop(0, pairs + n - 1, tick, 0)
+    vsum_ref[...] = held[5]
+    stores = []
+
+    def store(src, dst):
+        cp = pltpu.make_async_copy(src, dst, store_sem.at[len(stores)])
+        cp.start()
+        stores.append(cp)
+
+    down = gdown_ref.shape[0] // rows
+    up = down + gup_ref.shape[0] // rows
+    out = up + gout_ref.shape[0] // rows
+    cols = gqkv_ref.shape[2]
+    each = gqkv_ref.shape[1] * cols // (rows * gb.shape[3])
+    for i in range(chunks):
+        src = (rx if i % 2 == 0 else rb).at[i // 2]
+        for h in range(2):
+            at = rows // 2 * h
+            if i < down:
+                store(src.at[h], gdown_ref.at[pl.ds(i * rows + at, rows // 2), :])
+            elif i < up:
+                store(src.at[h], gup_ref.at[pl.ds((i - down) * rows + at, rows // 2), :])
+            elif i < out:
+                store(src.at[h], gout_ref.at[pl.ds((i - up) * rows + at, rows // 2), :])
+            else:
+                for j in range(gb.shape[3] // cols):
+                    row = ((i - out) % each * (gb.shape[3] // cols) + j) * rows + at
+                    store(
+                        src.at[h, :, pl.ds(j * cols, cols)],
+                        gqkv_ref.at[(i - out) // each, pl.ds(row, rows // 2), :],
+                    )
+    for cp in stores:
+        cp.wait()
+
+    def drain(k, carry):
+        reducer.drain(k)
+        return carry
+
+    lax.fori_loop(0, pairs, drain, 0)
+
+
+def run_sum(grads, vgrad, hidden, width, head_cols):
+    chunks, half = grads.shape[0], grads.shape[2]
+    pairs = chunks // 2
+    any_space = pl.BlockSpec(memory_space=pl.ANY)
+    vmem = pl.BlockSpec(memory_space=pltpu.VMEM)
+    dma = pltpu.SemaphoreType.DMA
+    low = lambda *shape: pltpu.VMEM(shape, LOW)
+    wide = lambda *shape: pltpu.VMEM(shape, F32)
+    return pl.pallas_call(
+        sum_kernel,
+        out_shape=(
+            jax.ShapeDtypeStruct((hidden, width), LOW),
+            jax.ShapeDtypeStruct((width, hidden), LOW),
+            jax.ShapeDtypeStruct((head_cols, width), LOW),
+            jax.ShapeDtypeStruct((3, width, head_cols), LOW),
+            jax.ShapeDtypeStruct(vgrad.shape, F32),
+        ),
+        in_specs=[any_space, vmem],
+        out_specs=(any_space,) * 4 + (vmem,),
+        scratch_shapes=[
+            low(chunks, 2, half, width),
+            low(pairs, 2, half, width),
+            low(pairs, half, width),
+            low(pairs, half, width),
+            low(pairs, 2, half, width),
+            low(pairs, half, width),
+            low(pairs, half, width),
+            wide(VECTOR_HOPS, *vgrad.shape),
+            wide(VECTOR_HOPS - 1, *vgrad.shape),
+            dma((pairs,)),
+            dma((chunks * 8,)),
+            dma((HOPS, pairs)),
+            dma((HOPS, pairs)),
+            dma((VECTOR_HOPS,)),
+            dma((VECTOR_HOPS,)),
+        ],
+        compiler_params=pltpu.CompilerParams(
+            collective_id=1, has_side_effects=True, vmem_limit_bytes=62 << 20
+        ),
+        name="gradient_sum",
+    )(grads, vgrad)
+
+
 def per_device(
     inputs,
     lengths,
@@ -507,32 +891,37 @@
         w_down,
         vec,
     )
-    grads = lax.psum(grads, "dp").astype(F32)
-    shared = lax.psum(vgrad[:6], ("dp", "tensor"))
-    split = lax.psum(vgrad[6:], "dp")
-    down = hidden // TILE
-    up = down + width // TILE
-    grad_down = grads[:down].reshape(hidden, width)
-    grad_up = grads[down:up].reshape(width, hidden)
-    grad_out = grads[up]
-    grad_qkv = grads[up + 1 :].reshape(3, TILE, width // TILE, head_cols)
-    grad_qkv = jnp.transpose(grad_qkv, (2, 1, 0, 3)).reshape(width, 3, head_cols)
+    if lax.axis_size("dp") == 8:
+        units = grads.reshape(-1, 2, UNIT // 2, width)
+        grad_down, grad_up, grad_out, grad_qkv, sums = run_sum(units, vgrad, hidden, width, head_cols)
+    else:
+        grads = lax.psum(grads, "dp")
+        sums = lax.psum(vgrad, "dp")
+        sums = jnp.concatenate([lax.psum(sums[:6], "tensor"), sums[6:]])
+        down = hidden // TILE
+        up = down + width // TILE
+        grad_down = grads[:down].reshape(hidden, width)
+        grad_up = grads[down:up].reshape(width, hidden)
+        grad_out = grads[up]
+        grad_qkv = grads[up + 1 :].reshape(3, TILE // UNIT, UNIT, width // head_cols, head_cols)
+        grad_qkv = jnp.transpose(grad_qkv, (0, 1, 3, 2, 4)).reshape(3, width, head_cols)
+    grad_qkv = jnp.transpose(grad_qkv.astype(F32), (1, 0, 2))
     return (
         output[None],
         grad_inputs[None],
         grad_qkv,
-        split[1, :head_cols],
-        split[1, head_cols : 2 * head_cols],
-        grad_out,
-        shared[0],
-        shared[1],
-        shared[2],
-        grad_up,
-        split[0],
-        grad_down,
-        shared[3],
-        shared[4],
-        shared[5],
+        sums[7, :head_cols],
+        sums[7, head_cols : 2 * head_cols],
+        grad_out.astype(F32),
+        sums[0],
+        sums[1],
+        sums[2],
+        grad_up.astype(F32),
+        sums[6],
+        grad_down.astype(F32),
+        sums[3],
+        sums[4],
+        sums[5],
     )
 
 

time: 405 us -> 310 us (0.77)
  waiting for transfers between devices: 150 us -> 0 us
  Pallas kernels: 149 us -> 288 us
  blocking collectives: 62.7 us -> 0 us
  local copies, waits for them, and re-layouts: 25.4 us -> 9.71 us
  between operations: 14.1 us -> 0.68 us
  other arithmetic: 2.85 us -> 11 us
    psum x1 -> x0, waiting for transfers between devices: 150 us -> none  [per_device(): grads = lax.psum(grads, 'dp').astype(F32)]
    pallas_call x0 -> x1, Pallas kernels: none -> 139 us  [run_sum(): pl.pallas_call(sum_kernel, out_shape=(jax.ShapeDtypeStruct((hidden, width...]
    psum x2 -> x0, blocking collectives: 62.7 us -> none  [the longest x1 39.7 us: per_device(): shared = lax.psum(vgrad[:6], ('dp', 'tensor'))]
    slice x6 -> x2, local copies, waits for them, and re-layouts: 9.7 us -> 3.07 us  [the longest x1 1.78 us: per_device(): sums[5]]
    convert_element_type x1 -> x3, other arithmetic: 1.55 us -> 7.78 us  [the longest x1 4.22 us: per_device(): grad_up.astype(F32)]
  transfers between devices with their start and end apart: 1 -> 0, of which waited for: 1 -> 0; matrix products, arithmetic and copies ran while one was open for 0% -> 0% of each run, Pallas kernels for 0% -> 0%
where the time goes in v3:
time: 310 us; the launch traced here: 309 us
  Pallas kernels  288 us (93%)
  other arithmetic  11 us (4%)
  local copies, waits for them, and re-layouts  9.71 us (3%)
    pallas_call x1, Pallas kernels, run_layer(): pl.pallas_call(layer_kernel, out_shape=(jax.ShapeDtypeStruct((batches, bl...  149 us
    pallas_call x1, Pallas kernels, run_sum(): pl.pallas_call(sum_kernel, out_shape=(jax.ShapeDtypeStruct((hidden, width...  139 us

profile of v3, /device:TPU:0, one launch (start us, length us, event | category | flops | bytes accessed | tf_op | source)
XLA Modules:
  0.0 309.4 jit_solution(2821119149089504318)
XLA Ops:
  0.7 0.7 pad_maximum_fusion
  1.3 0.7 stack.27
  2.0 0.7 stack.28
  2.7 0.7 stack.29
  3.4 0.7 stack.30
  4.1 0.7 stack.31
  4.8 0.7 stack.32
  5.5 0.7 stack.33
  6.1 0.1 stack.35
  6.2 0.6 convert_element_type.13.vec_ref
  6.8 149.2 %layer.1 = (bf16[3,128,1024]{2,1,0:T(8,128)(2,1)}, bf16[3,128,1024]{2,1,0:T(8,128)(2,1)}, bf16[12,256,1024]{2,1,0:T(8,128)(2,1)}, f32[8,1024]{1,0:T(8,128)}) custom-call(s32[1,3]{1,0:T(1,128)} %lengths_ref.1, bf16[3,128,1024]{2,1,0:T(8,128)(2,1)} %bitcast.21, bf16[3,128,1024]{2,1,0:T(8,128)(2,1)} %bitcast.22, bf16[3,1024,256]{2,1,0:T(8,128)(2,1)} %bitcast.18, ...), custom_call_target="tpu_custom_call" | custom-call | tf_op jit(solution)/shard_map/layer/pallas_call | solution.py:465
  156.0 138.8 %gradient_sum.1 = (bf16[1024,1024]{1,0:T(8,128)(2,1)}, bf16[1024,1024]{1,0:T(8,128)(2,1)}, bf16[256,1024]{1,0:T(8,128)(2,1)}, bf16[3,1024,256]{2,1,0:T(8,128)(2,1)}, f32[8,1024]{1,0:T(8,128)}) custom-call(bf16[48,2,32,1024]{3,2,1,0:T(8,128)(2,1)} %bitcast.17, f32[8,1024]{1,0:T(8,128)} %get-tuple-element.27.vgrad_ref), custom_call_target="tpu_custom_call" | custom-call | tf_op jit(solution)/shard_map/gradient_sum/pallas_call | solution.py:826
  294.9 1.8 fusion
  296.7 1.3 fusion.1
  297.9 0.0 copy-start
  297.9 4.2 %convert_element_type.15 = f32[1024,1024]{1,0:T(8,128)} convert(bf16[1024,1024]{1,0:T(8,128)(2,1)} %get-tuple-element.31) | non-fusion elementwise | flops 1048576 | bytes 6291456 | tf_op jit(solution)/shard_map/convert_element_type | solution.py:919
  302.2 0.0 copy-done
  302.2 0.0 copy-start.1
  302.2 2.5 convert_element_type.16
  304.6 0.0 copy-done.1
  304.6 0.0 copy-start.4
  304.6 0.0 copy-start.3
  304.6 1.9 convert_bitcast_fusion
  306.6 0.0 copy-start.2
  306.6 0.0 copy-done.4
  306.6 1.1 convert_element_type.14
  307.7 0.0 copy-done.3
  307.7 0.9 copy.33
  308.5 0.0 copy-done.2
  308.5 0.9 copy.34
  (2 shorter events, 0.0 us)
Async XLA Ops:
  297.9 4.2 %copy-start = (bf16[1024,1024]{1,0:T(8,128)(2,1)S(1)}, bf16[1024,1024]{1,0:T(8,128)(2,1)}, u32[]{:S(2)}) copy-start(bf16[1024,1024]{1,0:T(8,128)(2,1)} %get-tuple-element.32) | copy-start | bytes 6291460
  302.2 2.5 copy-start.1
  304.6 1.9 copy-start.4
  304.6 3.0 copy-start.3
  306.6 2.0 copy-start.2
